TPU v7x, 32 devices: a whole 2x2x4 slice. The times are simulated.
32 devices in a mesh: dp: 8 (over y, x, core), seq: 4 (over z).
Axes of the slice: x: 2, y: 2, z: 4, core: 2. Of those that a mesh axis runs over, the one named last changes fastest.
Arguments:
- patches: bfloat16 [12288, 128], P(('dp', 'seq')), parts along dimension 0, as said below
- pos_embed: bfloat16 [1536, 1024], P('seq'), may hold values from -3 to 3
- w_in: bfloat16 [128, 1024], replicated, may hold values from -0.5 to 0.5
- b_in: float32 [1024], replicated, may hold values from -3 to 3
- ln_gain: float32 [1024], replicated, may hold values from 0.5 to 1.5
- w_query: bfloat16 [1024, 1024], replicated, as said below
- w_key: bfloat16 [1024, 1024], replicated, as said below
- w_value: bfloat16 [1024, 1024], replicated, may hold values from -0.1875 to 0.1875
- w_proj: bfloat16 [1024, 1024], replicated, may hold values from -0.75 to 0.75
- out_gain: float32 [1024], replicated, may hold values from 0.5 to 1.5
- w_out: bfloat16 [1024, 256], replicated, may hold values from -0.09375 to 0.09375
- b_out: float32 [256], replicated, may hold values from -2 to 2
Outputs:
- latent: float32 [12288, 128], P(('dp', 'seq')), parts along dimension 0
- logdet: float32 [12288], P(('dp', 'seq')), parts along dimension 0
There are 8 independent parts, one for each index of `dp`. A program takes and returns all parts, laid end to end along the dimension named above; an argument that names none is the same for every part. Nothing has to cross between parts.
Inputs may be any that keep to these rules, and one draw needn't show every extreme that they name: real-valued patches. `w_query`: real-valued query weights. `w_key`: real-valued key weights.
All inputs are finite; a program needn't handle non-finite values.
Results may differ from a plain program's by a relative error of at most 0.0084.
Values may be sent and summed in bfloat16 or wider, within the bound.
No kernel may reach another device: no remote copies, remote signals or barrier semaphores. Data moves between devices by JAX's collectives and lax.ppermute only.
A program may use at most 128 MiB of HBM per device.

v0:
```python
import math

import jax
import jax.numpy as jnp
from jax import lax
from jax.sharding import PartitionSpec as P

H = 8


def from_behind(block, axis, distance):
    devices = range(lax.axis_size(axis))
    route = [(i - distance, i) for i in devices if i - distance in devices]
    return lax.ppermute(block, axis, route)


def normalize(values, gain):
    mean = jnp.mean(values, axis=-1, keepdims=True)
    centred = values - mean
    spread = jnp.mean(centred * centred, axis=-1, keepdims=True)
    return centred * lax.rsqrt(spread + 1e-05) * gain


def split_parts(array, count):
    return array.reshape((count, array.shape[0] // count) + array.shape[1:])


def join_parts(array):
    return array.reshape((array.shape[0] * array.shape[1],) + array.shape[2:])


def mirror_patches(patches, count):
    spread = lax.all_to_all(
        split_parts(patches, count), "seq", split_axis=0, concat_axis=0, tiled=True
    )
    collected = lax.all_to_all(spread[::-1], "seq", split_axis=0, concat_axis=0, tiled=True)
    return join_parts(collected)


def update_state(state, query_rows, query_pos, key_rows, value_rows, key_pos, scale):
    accum, top, total = state
    scores = (
        jnp.einsum("qhd,khd->qhk", query_rows, key_rows, preferred_element_type=jnp.float32) * scale
    )
    allowed = key_pos[None, None, :] <= query_pos[:, None, None]
    scores = jnp.where(allowed, scores, -1e30)
    new_top = jnp.maximum(top, jnp.max(scores, axis=2))
    weights = jnp.where(allowed, jnp.exp(scores - new_top[..., None]), 0.0)
    factor = jnp.exp(top - new_top)
    accum = accum * factor[..., None] + jnp.einsum(
        "qhk,khd->qhd", weights.astype(jnp.bfloat16), value_rows, preferred_element_type=jnp.float32
    )
    total = total * factor + jnp.sum(weights, axis=2)
    return (accum, new_top, total)


def shards(
    patches, pos_embed, w_in, b_in, ln_gain, w_query, w_key, w_value, w_proj, out_gain, w_out, b_out
):
    count = lax.axis_size("seq")
    index = lax.axis_index("seq")
    rows = patches.shape[0]
    feats = patches.shape[1]
    width = w_query.shape[0]
    head_size = width // H
    half = rows // 2
    mirrored = mirror_patches(patches, count)
    flipped = mirrored[::-1]
    previous = from_behind(flipped[rows - 1 :], "seq", 1)
    shifted = jnp.concatenate([previous, flipped[: rows - 1]], axis=0)
    local_pos = index * rows + jnp.arange(rows, dtype=jnp.int32)
    hidden = (
        jnp.dot(shifted, w_in, preferred_element_type=jnp.float32)
        + b_in
        + pos_embed.astype(jnp.float32)
    )
    normed = normalize(hidden, ln_gain).astype(jnp.bfloat16)
    queries = jnp.dot(normed, w_query, preferred_element_type=jnp.float32).astype(jnp.bfloat16)
    keys = jnp.dot(normed, w_key, preferred_element_type=jnp.float32).astype(jnp.bfloat16)
    values = jnp.dot(normed, w_value, preferred_element_type=jnp.float32).astype(jnp.bfloat16)
    scale = 1.0 / math.sqrt(head_size)
    query_heads = queries.reshape(rows, H, head_size)
    query_parts = (query_heads[:half], query_heads[half:])
    pos_parts = (local_pos[:half], local_pos[half:])

    def empty_state():
        return (
            jnp.zeros((half, H, head_size), jnp.float32),
            jnp.full((half, H), -1e30, jnp.float32),
            jnp.zeros((half, H), jnp.float32),
        )

    key_piece = lax.all_gather(keys, "seq", axis=0, tiled=True)
    value_piece = lax.all_gather(values, "seq", axis=0, tiled=True)
    length = key_piece.shape[0]
    block = 512
    piece_pos = jnp.arange(length, dtype=jnp.int32)

    def one_block(step, states):
        offset = step * block
        key_rows = lax.dynamic_slice_in_dim(key_piece, offset, block, 0).reshape(
            block, H, head_size
        )
        value_rows = lax.dynamic_slice_in_dim(value_piece, offset, block, 0).reshape(
            block, H, head_size
        )
        key_pos = lax.dynamic_slice_in_dim(piece_pos, offset, block, 0)
        updated = []
        for part_index in range(2):
            query_rows = query_parts[part_index]
            rows_pos = pos_parts[part_index]
            needed = jnp.min(key_pos) <= jnp.max(rows_pos)
            updated.append(
                lax.cond(
                    needed,
                    lambda s: update_state(
                        s, query_rows, rows_pos, key_rows, value_rows, key_pos, scale
                    ),
                    lambda s: s,
                    states[part_index],
                )
            )
        return (updated[0], updated[1])

    states = lax.fori_loop(0, length // block, one_block, (empty_state(), empty_state()))
    outputs = []
    for part_index in range(2):
        accum, top, total = states[part_index]
        outputs.append((accum / total[..., None]).reshape(half, width))
    attended = jnp.concatenate(outputs, axis=0).astype(jnp.bfloat16)
    mixed = hidden + jnp.dot(attended, w_proj, preferred_element_type=jnp.float32)
    second = normalize(mixed, out_gain).astype(jnp.bfloat16)
    stats = jnp.dot(second, w_out, preferred_element_type=jnp.float32) + b_out
    shift_part = stats[:, :feats]
    log_scale = stats[:, feats:]
    latent = (flipped.astype(jnp.float32) - shift_part) * jnp.exp(-log_scale)
    logdet = -jnp.mean(log_scale, axis=1)
    return (latent, logdet)


def solution(mesh):
    in_specs = (
        P(("dp", "seq"), None),
        P("seq", None),
        P(),
        P(),
        P(),
        P(),
        P(),
        P(),
        P(),
        P(),
        P(),
        P(),
    )
    out_specs = (P(("dp", "seq"), None), P(("dp", "seq")))
    return jax.shard_map(shards, mesh=mesh, in_specs=in_specs, out_specs=out_specs, check_vma=False)
```

profile of v0, /device:TPU:27, one launch (start us, length us, event | category | flops | bytes accessed | tf_op | source)
XLA Modules:
  0.0 249.5 jit_solution(16186625544420172401)
XLA Ops:
  7.2 7.4 %all_to_all.10 = bf16[4,96,128]{2,1,0:T(8,128)(2,1)S(1)} all-to-all(bf16[4,96,128]{2,1,0:T(8,128)(2,1)} %bitcast.86), channel_id=1, replica_groups=mesh['dp'=8,'seq'=4] {'seq'}, dimensions={0} | all-to-all | bytes 196608 | tf_op jit(solution)/shard_map/all_to_all | solution.py:33
  14.7 6.8 %all_to_all.11 = bf16[4,96,128]{2,1,0:T(8,128)(2,1)S(1)} all-to-all(bf16[4,96,128]{2,1,0:T(8,128)(2,1)S(1)} %rev.6), channel_id=1, replica_groups=mesh['dp'=8,'seq'=4] {'seq'}, dimensions={0} | all-to-all | bytes 196608 | tf_op jit(solution)/shard_map/all_to_all | solution.py:36
  21.5 1.3 collective-permute-start
  23.2 2.6 %collective-permute-done = bf16[1,128]{1,0:T(2,128)(2,1)S(1)} collective-permute-done((bf16[1,128]{1,0:T(2,128)(2,1)S(1)}, bf16[1,128]{1,0:T(2,128)(2,1)S(1)}, u32[]{:S(2)}, u32[]{:S(2)}) %collective-permute-start) | collective-permute-done | bytes 288 | tf_op jit(solution)/shard_map/ppermute | solution.py:14
  25.8 1.6 fusion.53
  29.6 2.0 convolution_convert_fusion.2
  31.6 3.5 %convolution_convert_fusion.1 = bf16[384,1024]{1,0:T(8,128)(2,1)} fusion(bf16[384,1024]{1,0:T(8,128)(2,1)S(1)} %multiply_convert_fusion.1, bf16[1024,1024]{1,0:T(8,128)(2,1)} %param.25), kind=kOutput, calls=%fused_computation.47 | convolution fusion | flops 805699584 | bytes 3670016 | tf_op jit(solution)/shard_map/dot_general | solution.py:80
  35.2 1.4 slice_reduce_fusion.1
  36.7 1.4 rev.7
  38.1 2.6 %convolution_convert_fusion = bf16[384,1024]{1,0:T(8,128)(2,1)S(1)} fusion(bf16[384,1024]{1,0:T(8,128)(2,1)S(1)} %multiply_convert_fusion.1, bf16[1024,1024]{1,0:T(8,128)(2,1)} %param.23), kind=kOutput, calls=%fused_computation.46 | convolution fusion | flops 805699584 | bytes 3670016 | tf_op jit(solution)/shard_map/dot_general | solution.py:78
  41.7 55.8 %all-gather.3.cloned.1.call-done = bf16[1536,1024]{1,0:T(8,128)(2,1)} async-done(((bf16[384,1024]{1,0:T(8,128)(2,1)}), bf16[1536,1024]{1,0:T(8,128)(2,1)}) %all-gather.3.cloned.1.call-update) | async-done | bytes 3145744 | tf_op jit(solution)/shard_map/all_gather | solution.py:93
  97.5 63.8 %all-gather.5.cloned.1.call-done = bf16[1536,1024]{1,0:T(8,128)(2,1)} async-done(((bf16[384,1024]{1,0:T(8,128)(2,1)}), bf16[1536,1024]{1,0:T(8,128)(2,1)}) %all-gather.5.cloned.1.call-update) | async-done | bytes 3145744 | tf_op jit(solution)/shard_map/all_gather | solution.py:94
  164.9 71.1 %while.24 = (s32[]{:T(128)}, f32[192,8,128]{2,0,1:T(8,128)}, f32[192,8]{0,1:T(8,128)S(1)}, f32[192,8]{0,1:T(8,128)}, f32[192,8,128]{2,0,1:T(8,128)}, /*index=5*/...) while((s32[]{:T(128)}, f32[192,8,128]{2,0,1:T(8,128)}, ...), condition=%wide.region_14.15_spmd, body=%wide.region_4.14_spmd.sunk | while | flops 826743296 | bytes 57452816 | solution.py:125
  164.9 2.0 fusion.73
  169.4 3.2 %constant_dynamic-slice_fusion.3 = (bf16[512,1024]{1,0:T(8,128)(2,1)}, bf16[512,1024]{1,0:T(8,128)(2,1)}) fusion(bf16[1536,1024]{1,0:T(8,128)(2,1)} %get-tuple-element.676, s32[]{:T(128)S(6)} %select_n.72, bf16[1536,1024]{1,0:T(8,128)(2,1)} %get-tuple-element.675), kind=kLoop, calls=%fused_computation.38.clone.1 | loop fusion | bytes 4194308 | tf_op jit(solution)/shard_map/while/body/eval_jaxpr/dynamic_slice | solution.py:104
  172.6 1.5 copy.46
  174.1 2.3 copy.47
  176.5 6.7 %conditional.4 = ((f32[192,8,128]{2,0,1:T(8,128)}, f32[192,8]{0,1:T(8,128)S(1)}, f32[192,8]{0,1:T(8,128)})) conditional(s32[]{:T(128)} %convert_element_type.73, (f32[192,8,128]{2,0,1:T(8,128)}, f32[192,8]{0,1:T(8,128)S(1)}, f32[192,8]{0,1:T(8,128)}) %tuple.78, (s32[512]{0:T(512)}, s32[192]{0:T(256)}, bf16[512,8,128]{0,2,1:T(8,128)(2,1)S(1)}, ...), branch_computations={%region_6.6_spmd, %region_7.9_spmd} | conditional | flops 413371392 | bytes 24529836 | solution.py:114
  177.3 1.8 fusion
  179.1 1.1 fusion.1
  180.8 1.5 fusion.13
  183.2 5.4 %conditional.5 = ((f32[192,8,128]{2,0,1:T(8,128)}, f32[192,8]{0,1:T(8,128)S(1)}, f32[192,8]{0,1:T(8,128)})) conditional(s32[]{:T(128)} %convert_element_type.74, (f32[192,8,128]{2,0,1:T(8,128)}, f32[192,8]{0,1:T(8,128)S(1)}, f32[192,8]{0,1:T(8,128)}) %tuple.80, (s32[512]{0:T(512)}, s32[192]{0:T(256)}, bf16[512,8,128]{0,2,1:T(8,128)(2,1)S(1)}, ...), branch_computations={%region_10.10_spmd, %region_11.13_spmd} | conditional | flops 413371392 | bytes 24529836 | solution.py:114
  184.8 1.1 fusion.20
  186.3 1.5 fusion.32
  188.6 2.0 fusion.73
  193.2 3.2 %constant_dynamic-slice_fusion.3 = (bf16[512,1024]{1,0:T(8,128)(2,1)}, bf16[512,1024]{1,0:T(8,128)(2,1)}) fusion(bf16[1536,1024]{1,0:T(8,128)(2,1)} %get-tuple-element.676, s32[]{:T(128)S(6)} %select_n.72, bf16[1536,1024]{1,0:T(8,128)(2,1)} %get-tuple-element.675), kind=kLoop, calls=%fused_computation.38.clone.1 | loop fusion | bytes 4194308 | tf_op jit(solution)/shard_map/while/body/eval_jaxpr/dynamic_slice | solution.py:104
  196.3 1.5 copy.46
  197.8 2.3 copy.47
  200.2 6.7 %conditional.4 = ((f32[192,8,128]{2,0,1:T(8,128)}, f32[192,8]{0,1:T(8,128)S(1)}, f32[192,8]{0,1:T(8,128)})) conditional(s32[]{:T(128)} %convert_element_type.73, (f32[192,8,128]{2,0,1:T(8,128)}, f32[192,8]{0,1:T(8,128)S(1)}, f32[192,8]{0,1:T(8,128)}) %tuple.78, (s32[512]{0:T(512)}, s32[192]{0:T(256)}, bf16[512,8,128]{0,2,1:T(8,128)(2,1)S(1)}, ...), branch_computations={%region_6.6_spmd, %region_7.9_spmd} | conditional | flops 413371392 | bytes 24529836 | solution.py:114
  201.0 1.8 fusion
  202.8 1.1 fusion.1
  204.5 1.5 fusion.13
  206.9 5.4 %conditional.5 = ((f32[192,8,128]{2,0,1:T(8,128)}, f32[192,8]{0,1:T(8,128)S(1)}, f32[192,8]{0,1:T(8,128)})) conditional(s32[]{:T(128)} %convert_element_type.74, (f32[192,8,128]{2,0,1:T(8,128)}, f32[192,8]{0,1:T(8,128)S(1)}, f32[192,8]{0,1:T(8,128)}) %tuple.80, (s32[512]{0:T(512)}, s32[192]{0:T(256)}, bf16[512,8,128]{0,2,1:T(8,128)(2,1)S(1)}, ...), branch_computations={%region_10.10_spmd, %region_11.13_spmd} | conditional | flops 413371392 | bytes 24529836 | solution.py:114
  208.5 1.1 fusion.20
  210.0 1.5 fusion.32
  212.3 2.0 fusion.73
  216.9 3.2 %constant_dynamic-slice_fusion.3 = (bf16[512,1024]{1,0:T(8,128)(2,1)}, bf16[512,1024]{1,0:T(8,128)(2,1)}) fusion(bf16[1536,1024]{1,0:T(8,128)(2,1)} %get-tuple-element.676, s32[]{:T(128)S(6)} %select_n.72, bf16[1536,1024]{1,0:T(8,128)(2,1)} %get-tuple-element.675), kind=kLoop, calls=%fused_computation.38.clone.1 | loop fusion | bytes 4194308 | tf_op jit(solution)/shard_map/while/body/eval_jaxpr/dynamic_slice | solution.py:104
  220.0 1.5 copy.46
  221.5 2.3 copy.47
  223.9 6.7 %conditional.4 = ((f32[192,8,128]{2,0,1:T(8,128)}, f32[192,8]{0,1:T(8,128)S(1)}, f32[192,8]{0,1:T(8,128)})) conditional(s32[]{:T(128)} %convert_element_type.73, (f32[192,8,128]{2,0,1:T(8,128)}, f32[192,8]{0,1:T(8,128)S(1)}, f32[192,8]{0,1:T(8,128)}) %tuple.78, (s32[512]{0:T(512)}, s32[192]{0:T(256)}, bf16[512,8,128]{0,2,1:T(8,128)(2,1)S(1)}, ...), branch_computations={%region_6.6_spmd, %region_7.9_spmd} | conditional | flops 413371392 | bytes 24529836 | solution.py:114
  224.7 1.8 fusion
  226.5 1.1 fusion.1
  228.2 1.5 fusion.13
  230.6 5.4 %conditional.5 = ((f32[192,8,128]{2,0,1:T(8,128)}, f32[192,8]{0,1:T(8,128)S(1)}, f32[192,8]{0,1:T(8,128)})) conditional(s32[]{:T(128)} %convert_element_type.74, (f32[192,8,128]{2,0,1:T(8,128)}, f32[192,8]{0,1:T(8,128)S(1)}, f32[192,8]{0,1:T(8,128)}) %tuple.80, (s32[512]{0:T(512)}, s32[192]{0:T(256)}, bf16[512,8,128]{0,2,1:T(8,128)(2,1)S(1)}, ...), branch_computations={%region_10.10_spmd, %region_11.13_spmd} | conditional | flops 413371392 | bytes 24529836 | solution.py:114
  232.2 1.1 fusion.20
  233.7 1.5 fusion.32
  236.1 1.5 copy_bitcast_fusion
  237.6 1.4 copy_bitcast_fusion.1
  (136 shorter events, 26.2 us)
Async XLA Ops:
  7.2 231.8 %copy-start = (bf16[1024,1024]{1,0:T(8,128)(2,1)S(1)}, bf16[1024,1024]{1,0:T(8,128)(2,1)}, u32[]{:S(2)}) copy-start(bf16[1024,1024]{1,0:T(8,128)(2,1)} %param.26) | copy-start | bytes 6291460
  7.2 90.3 %all-gather.3.cloned.1.call-start = ((), (), s32[]{:S(2)}) async-start(), calls=%async_computation.2 | async-start | bytes 3932160 | tf_op jit(solution)/shard_map/all_gather | solution.py:93
  21.5 4.3 %collective-permute-start = (bf16[1,128]{1,0:T(2,128)(2,1)S(1)}, bf16[1,128]{1,0:T(2,128)(2,1)S(1)}, u32[]{:S(2)}, u32[]{:S(2)}) collective-permute-start(bf16[1,128]{1,0:T(2,128)(2,1)S(1)} %slice.45), channel_id=1, source_target_pairs={{0,1},{1,2},{2,3},{4,5},{5,6},{6,7},{8,9},{9,10},{10,11},{12,13},{... | collective-permute-start | bytes 776 | tf_op jit(solution)/shard_map/ppermute | solution.py:14
  23.1 5.4 %copy-start.15 = (f32[1024]{0:T(1024)S(1)}, f32[1024]{0:T(1024)}, u32[]{:S(2)}) copy-start(f32[1024]{0:T(1024)} %param.22) | copy-start | bytes 12292
  27.4 1.2 copy-start.3
  27.4 2.2 copy-start.18
  31.6 129.7 %all-gather.5.cloned.1.call-start = ((), (), s32[]{:S(2)}) async-start(), calls=%async_computation.3 | async-start | bytes 3932160 | tf_op jit(solution)/shard_map/all_gather | solution.py:94
  179.1 1.1 copy-start.12
  179.1 1.7 copy-start.1
  179.1 1.7 copy-start.7
  180.2 0.6 copy-start.13
  182.3 0.9 copy-start.8
  184.8 1.1 copy-start.10
  184.8 1.2 copy-start.2
  184.8 1.4 copy-start.5
  185.9 1.8 copy-start.11
  187.7 0.9 copy-start.6
  202.8 1.1 copy-start.12
  202.8 1.7 copy-start.1
  202.8 1.7 copy-start.7
  203.9 0.6 copy-start.13
  206.0 0.9 copy-start.8
  208.5 1.1 copy-start.10
  208.5 1.2 copy-start.2
  208.5 1.4 copy-start.5
  209.7 1.8 copy-start.11
  211.5 0.9 copy-start.6
  226.5 1.1 copy-start.12
  226.5 1.7 copy-start.1
  226.5 1.7 copy-start.7
  227.6 0.6 copy-start.13
  229.7 0.9 copy-start.8
  232.2 1.1 copy-start.10
  232.2 1.2 copy-start.2
  232.2 1.4 copy-start.5
  233.4 1.8 copy-start.11
  235.2 0.9 copy-start.6
  236.1 3.0 %copy-start.4 = (f32[384,1024]{1,0:T(8,128)S(1)}, f32[384,1024]{1,0:T(8,128)}, u32[]{:S(2)}) copy-start(f32[384,1024]{1,0:T(8,128)} %copy-done.3) | copy-start | bytes 4718596
  239.0 1.5 copy-start.9
  239.0 1.5 copy-start.16
  239.1 1.5 copy-start.17
  240.2 1.0 copy-start.14
Sparse Core Ops, SparseCore 0:
  31.7 65.7 all-gather.2
  99.0 62.1 all-gather.4
where the time goes:
time: 251 us; the launch traced here: 249 us
  waiting for transfers between devices  122 us (49%)
  local copies, waits for them, and re-layouts  38.1 us (15%)
  matrix products  27.9 us (11%)
  other arithmetic  23.3 us (9%)
  blocking collectives  14.3 us (6%)
  between operations  14.3 us (6%)
  loops' own time  8.15 us (3%)
    all_gather x1, waiting for transfers between devices, shards(): value_piece = lax.all_gather(values, 'seq', axis=0, tiled=True)  63.8 us
    all_gather x1, waiting for transfers between devices, shards(): key_piece = lax.all_gather(keys, 'seq', axis=0, tiled=True)  55.8 us
    dynamic_slice x6, local copies, waits for them, and re-layouts, one_block(): lax.dynamic_slice_in_dim(value_piece, offset, block, 0)  16.6 us
    dot_general x6, matrix products, update_state(): jnp.einsum('qhk,khd->qhd', weights.astype(jnp.bfloat16), value_rows, pref...  8.86 us
    cond x66, local copies, waits for them, and re-layouts  8.02 us
    another operation x1, loops' own time, shards(): lax.fori_loop(0, length // block, one_block, (empty_state(), empty_state()))  7.63 us
    dot_general x6, matrix products, update_state(): jnp.einsum('qhd,khd->qhk', query_rows, key_rows, preferred_element_type=j...  7.59 us
    all_to_all x1, blocking collectives, mirror_patches(): lax.all_to_all(split_parts(patches, count), 'seq', split_axis=0, concat_a...  7.44 us
  transfers between devices with their start and end apart: 3, of which 3 were waited for; matrix products, arithmetic and copies ran while one was open for 4% of the time, Pallas kernels for 0%

commit v1 on v0

v1 whole, which is shorter than its diff:
```python
import functools
import math

import jax
import jax.numpy as jnp
from jax import lax
from jax.experimental import pallas as pl
from jax.experimental.pallas import tpu as pltpu
from jax.sharding import PartitionSpec as P

H = 8
LANES = 128
PAD = 16
F32 = jnp.float32
BF16 = jnp.bfloat16
VMEM = pltpu.VMEM


def dot(a, b):
    return jnp.dot(a, b, preferred_element_type=F32)


def normalize(values, gain):
    mean = jnp.mean(values, axis=-1, keepdims=True)
    centred = values - mean
    spread = jnp.mean(centred * centred, axis=-1, keepdims=True)
    return centred * lax.rsqrt(spread + 1e-05) * gain


def place_patches(slots, refs, held, rows, me):
    if slots is None:
        held[: held.shape[0] - PAD] = refs[0][...]
    else:
        for slot, ref in zip(slots, refs):
            start = pl.multiple_of(jnp.bitwise_xor(me, slot) * rows, rows)
            held[pl.ds(start, rows)] = ref[...]
    held[held.shape[0] - PAD :] = jnp.zeros((PAD, held.shape[1]), BF16)


def window(held, block, rows, count):
    start = pl.multiple_of((count - 1 - block) * rows, rows)
    return held[pl.ds(start, rows + PAD)]


def reverse(part, last):
    rows = part.shape[0] - PAD
    row = lax.broadcasted_iota(jnp.int32, (rows, rows + PAD), 0)
    col = lax.broadcasted_iota(jnp.int32, (rows, rows + PAD), 1)
    return dot((row + col == last).astype(BF16), part)


def hidden_of(part, pos, w_in, b_in):
    rows = part.shape[0] - PAD
    shifted = reverse(part, rows).astype(BF16)
    return dot(shifted, w_in) + b_in + pos.astype(F32)


def scores_of(queries, keys):
    return lax.dot_general(queries, keys, (((1,), (1,)), ((), ())), preferred_element_type=F32)


def repeat(column, width):
    return jnp.concatenate([column] * (width // LANES), axis=1)


def with_ones(values):
    return jnp.concatenate([values, jnp.ones((values.shape[0], LANES), BF16)], axis=1)


def own_kernel(
    slots, count, n_patch, *refs
):
    patch_refs = refs[:n_patch]
    (pos, w_in, b_in, gain, w_query, w_key, w_value) = refs[n_patch : n_patch + 7]
    (hidden_out, query_out, acc_out, top_out, held) = refs[n_patch + 7 :]
    rows = pos.shape[0]
    head = w_query.shape[1] // H
    me = lax.axis_index("seq")
    place_patches(slots, patch_refs, held, rows, me)
    hidden = hidden_of(window(held, me, rows, count), pos[...], w_in[...], b_in[...])
    hidden_out[...] = hidden
    normed = normalize(hidden, gain[...]).astype(BF16)
    scale = math.log2(math.e) / math.sqrt(head)
    query_out[...] = (dot(normed, w_query[...]) * scale).astype(BF16)
    keys = dot(normed, w_key[...]).astype(BF16)
    values = dot(normed, w_value[...]).astype(BF16)
    row = lax.broadcasted_iota(jnp.int32, (rows, rows), 0)
    col = lax.broadcasted_iota(jnp.int32, (rows, rows), 1)
    allowed = col <= row
    for h in range(H):
        part = slice(h * head, (h + 1) * head)
        scores = jnp.where(allowed, scores_of(query_out[:, part], keys[:, part]), -1e30)
        top = jnp.broadcast_to(jnp.max(scores, axis=1, keepdims=True), (rows, LANES))
        weights = jnp.exp2(scores - repeat(top, rows)).astype(BF16)
        top_out[h] = top
        acc_out[h] = dot(weights, with_ones(values[:, part]))


def rest_kernel(slots, count, n_patch, n_pos, *refs):
    patch_refs = refs[:n_patch]
    pos_refs = refs[n_patch : n_patch + n_pos]
    (hidden, query, acc_in, top_in, w_in, b_in, gain, w_key, w_value, w_proj, out_gain, w_out, b_out) = refs[
        n_patch + n_pos : n_patch + n_pos + 13
    ]
    (latent_out, logdet_out, held, pos_held, acc, top) = refs[n_patch + n_pos + 13 :]
    rows, width = hidden.shape
    head = width // H
    feats = patch_refs[0].shape[1]
    me = lax.axis_index("seq")
    place_patches(slots, patch_refs, held, rows, me)
    acc[...] = acc_in[...]
    top[...] = top_in[...]
    if slots is not None:
        group = lax.axis_index("dp")
        for piece, ref in enumerate(pos_refs):
            pos_held[jnp.bitwise_xor(group, piece)] = ref[...]

    def add_block(block, pos):
        hid = hidden_of(window(held, block, rows, count), pos, w_in[...], b_in[...])
        normed = normalize(hid, gain[...]).astype(BF16)
        keys = dot(normed, w_key[...]).astype(BF16)
        values = dot(normed, w_value[...]).astype(BF16)
        for h in range(H):
            part = slice(h * head, (h + 1) * head)
            scores = scores_of(query[:, part], keys[:, part])
            old = top[h]
            new = jnp.maximum(old, jnp.max(scores, axis=1, keepdims=True))
            weights = jnp.exp2(scores - repeat(new, rows)).astype(BF16)
            factor = jnp.exp2(old - new)
            top[h] = new
            acc[h] = acc[h] * repeat(factor, head + LANES) + dot(weights, with_ones(values[:, part]))

    if slots is None:

        def step(block, carry):
            add_block(block, pos_refs[0][block])
            return carry

        lax.fori_loop(0, me, step, 0)
    else:
        for place in range(count - 1):
            block = jnp.bitwise_xor(me, place + 1)

            @pl.when(block < me)
            def _():
                chunks = [pos_held[c, place * rows : (place + 1) * rows] for c in range(pos_held.shape[0])]
                add_block(block, jnp.concatenate(chunks, axis=1))

    attended = jnp.concatenate([(acc[h][:, :head] / acc[h][:, head:]).astype(BF16) for h in range(H)], axis=1)
    mixed = hidden[...] + dot(attended, w_proj[...])
    second = normalize(mixed, out_gain[...]).astype(BF16)
    stats = dot(second, w_out[...]) + b_out[...]
    shift_part = stats[:, :feats]
    log_scale = stats[:, feats:]
    flipped = reverse(window(held, me, rows, count), rows - 1)
    latent_out[...] = (flipped - shift_part) * jnp.exp(-log_scale)
    logdet_out[...] = -jnp.mean(jnp.transpose(log_scale), axis=0, keepdims=True)


def spec(n):
    return [pl.BlockSpec(memory_space=VMEM)] * n


def shards(
    patches, pos_embed, w_in, b_in, ln_gain, w_query, w_key, w_value, w_proj, out_gain, w_out, b_out
):
    count = lax.axis_size("seq")
    groups = lax.axis_size("dp")
    rows, feats = patches.shape
    width = w_query.shape[0]
    head = width // H
    b_in, ln_gain, out_gain, b_out = [a.reshape(1, -1) for a in (b_in, ln_gain, out_gain, b_out)]
    quick = count == 4 and groups == 8 and width == groups * LANES
    if quick:
        group = lax.axis_index("dp")
        cut = lax.dynamic_slice_in_dim(pos_embed, group * LANES, LANES, 1)

        def swap(block, axis, mask, size):
            return lax.ppermute(block, axis, [(i, i ^ mask) for i in range(size)])

        along = [swap(cut, "seq", m, count) for m in (1, 2, 3)]
        slots = (0, 1, 2, 3)
        patch_list = [patches] + [swap(patches, "seq", m, count) for m in (1, 2, 3)]
        mine = jnp.concatenate(along, axis=0)
        plane = [mine] + [swap(mine, "dp", m, groups) for m in (2, 4, 6)]
        other = [swap(block, "dp", 1, groups) for block in plane]
        pos_list = []
        for a, b in zip(plane, other):
            pos_list += [a, b]
        own_slots = (0, 2, 3)
        own_patches = [patch_list[s] for s in own_slots]
    else:
        slots = own_slots = None
        patch_list = own_patches = [lax.all_gather(patches, "seq", axis=0, tiled=True)]
        pos_list = [lax.all_gather(pos_embed, "seq", axis=0, tiled=False)]
    held = VMEM((count * rows + PAD, feats), BF16)
    own = pl.pallas_call(
        functools.partial(own_kernel, own_slots, count, len(own_patches)),
        out_shape=(
            jax.ShapeDtypeStruct((rows, width), F32),
            jax.ShapeDtypeStruct((rows, width), BF16),
            jax.ShapeDtypeStruct((H, rows, head + LANES), F32),
            jax.ShapeDtypeStruct((H, rows, LANES), F32),
        ),
        in_specs=spec(len(own_patches) + 7),
        out_specs=spec(4),
        scratch_shapes=[held],
        compiler_params=pltpu.CompilerParams(vmem_limit_bytes=24 << 20),
        cost_estimate=pl.CostEstimate(flops=6 << 30, bytes_accessed=12 << 20, transcendentals=0),
        name="own_block",
    )(*own_patches, pos_embed, w_in, b_in, ln_gain, w_query, w_key, w_value)
    hidden, query, acc, top = own
    pos_shape = (groups, (count - 1) * rows, LANES) if quick else (8, LANES)
    latent, logdet = pl.pallas_call(
        functools.partial(rest_kernel, slots, count, len(patch_list), len(pos_list)),
        out_shape=(
            jax.ShapeDtypeStruct((rows, feats), F32),
            jax.ShapeDtypeStruct((1, rows), F32),
        ),
        in_specs=spec(len(patch_list) + len(pos_list) + 13),
        out_specs=spec(2),
        scratch_shapes=[
            held,
            VMEM(pos_shape, BF16),
            VMEM((H, rows, head + LANES), F32),
            VMEM((H, rows, LANES), F32),
        ],
        compiler_params=pltpu.CompilerParams(vmem_limit_bytes=24 << 20),
        cost_estimate=pl.CostEstimate(flops=12 << 30, bytes_accessed=16 << 20, transcendentals=0),
        name="rest_blocks",
    )(*patch_list, *pos_list, hidden, query, acc, top, w_in, b_in, ln_gain, w_key, w_value, w_proj, out_gain, w_out, b_out)
    return (latent, logdet.reshape(rows))


def solution(mesh):
    in_specs = (
        P(("dp", "seq"), None),
        P("seq", None),
        P(),
        P(),
        P(),
        P(),
        P(),
        P(),
        P(),
        P(),
        P(),
        P(),
    )
    out_specs = (P(("dp", "seq"), None), P(("dp", "seq")))
    return jax.shard_map(shards, mesh=mesh, in_specs=in_specs, out_specs=out_specs, check_vma=False)
```

time: 251 us -> 63.8 us (0.25)
  waiting for transfers between devices: 122 us -> 19.9 us
  local copies, waits for them, and re-layouts: 38.1 us -> 10.1 us
  matrix products: 27.9 us -> 0 us
  Pallas kernels: 0 us -> 23.7 us
  other arithmetic: 23.3 us -> 0.6 us
  blocking collectives: 14.3 us -> 0 us
  between operations: 14.3 us -> 0.79 us
  loops' own time: 8.15 us -> 0 us
  starting transfers between devices: 1.36 us -> 8.3 us
    all_gather x2 -> x0, waiting for transfers between devices: 120 us -> none  [the longest x1 63.8 us: shards(): value_piece = lax.all_gather(values, 'seq', axis=0, tiled=True)]
    dot_general x18 -> x0, matrix products: 27.9 us -> none  [the longest x6 8.86 us: update_state(): jnp.einsum('qhk,khd->qhd', weights.astype(jnp.bfloat16), value_rows, pref...]
    pallas_call x0 -> x2, Pallas kernels: none -> 23.7 us  [the longest x1 18.1 us: shards(): pl.pallas_call(functools.partial(rest_kernel, slots, count, len(patch_lis...]
    dynamic_slice x9 -> x1, local copies, waits for them, and re-layouts: 21 us -> 0.9 us  [shards(): cut = lax.dynamic_slice_in_dim(pos_embed, group * LANES, LANES, 1)]
    ppermute x1 -> x13, waiting for transfers between devices: 2.61 us -> 19.9 us  [swap(): return lax.ppermute(block, axis, [(i, i ^ mask) for i in range(size)])]
    all_to_all x2 -> x0, blocking collectives: 14.3 us -> none  [the longest x1 7.44 us: mirror_patches(): lax.all_to_all(split_parts(patches, count), 'seq', split_axis=0, concat_a...]
    another operation x7 -> x0, loops' own time: 8.15 us -> none  [the longest x1 7.63 us: shards(): lax.fori_loop(0, length // block, one_block, (empty_state(), empty_state()))]
    cond x66 -> x0, local copies, waits for them, and re-layouts: 8.02 us -> none
  transfers between devices with their start and end apart: 3 -> 13, of which waited for: 3 -> 5; matrix products, arithmetic and copies ran while one was open for 4% -> 0% of each run, Pallas kernels for 0% -> 9%
where the time goes in v1:
time: 63.8 us; the launch traced here: 63.4 us
  Pallas kernels  23.7 us (37%)
  waiting for transfers between devices  19.9 us (31%)
  local copies, waits for them, and re-layouts  10.1 us (16%)
  starting transfers between devices  8.3 us (13%)
  between operations  0.79 us (1%)
    ppermute x13, waiting for transfers between devices, swap(): return lax.ppermute(block, axis, [(i, i ^ mask) for i in range(size)])  19.9 us
    pallas_call x1, Pallas kernels, shards(): pl.pallas_call(functools.partial(rest_kernel, slots, count, len(patch_lis...  18.1 us
    unnamed x30, local copies, waits for them, and re-layouts  9.17 us
    ppermute x13, starting transfers between devices, swap(): return lax.ppermute(block, axis, [(i, i ^ mask) for i in range(size)])  8.3 us
    pallas_call x1, Pallas kernels, shards(): pl.pallas_call(functools.partial(own_kernel, own_slots, count, len(own_pa...  5.58 us
  transfers between devices with their start and end apart: 13, of which 5 were waited for; matrix products, arithmetic and copies ran while one was open for 0% of the time, Pallas kernels for 9%

profile of v1, /device:TPU:27, one launch (start us, length us, event | category | flops | bytes accessed | tf_op | source)
XLA Modules:
  0.0 63.4 jit_solution(1561175952666828565)
XLA Ops:
  0.6 0.9 %constant_dynamic-slice_fusion = bf16[384,128]{1,0:T(8,128)(2,1)S(1)} fusion(bf16[384,1024]{1,0:T(8,128)(2,1)} %refs_3_.1, s32[]{:T(128)S(6)} %select_n.3), kind=kLoop, calls=%fused_computation.3 | loop fusion | bytes 196612 | tf_op jit(solution)/shard_map/dynamic_slice | solution.py:176
  1.5 0.2 collective-permute-start.3
  1.7 1.1 %collective-permute-start.5 = (bf16[384,128]{1,0:T(8,128)(2,1)S(1)}, bf16[384,128]{1,0:T(8,128)(2,1)S(1)}, u32[]{:S(2)}, u32[]{:S(2)}) collective-permute-start(bf16[384,128]{1,0:T(8,128)(2,1)S(1)} %constant_dynamic-slice_fusion), channel_id=1, source_target_pairs={{0,3},{1,2},{2,1},{3,0},{4,7},{5,6},{6,5},{7,4},{8,11},{9,10},{10,... | collective-permute-start | bytes 294920 | tf_op jit(solution)/shard_map/ppermute | solution.py:179
  2.8 1.4 %collective-permute-start.4 = (bf16[384,128]{1,0:T(8,128)(2,1)S(1)}, bf16[384,128]{1,0:T(8,128)(2,1)S(1)}, u32[]{:S(2)}, u32[]{:S(2)}) collective-permute-start(bf16[384,128]{1,0:T(8,128)(2,1)S(1)} %constant_dynamic-slice_fusion), channel_id=1, source_target_pairs={{0,2},{1,3},{2,0},{3,1},{4,6},{5,7},{6,4},{7,5},{8,10},{9,11},{10,... | collective-permute-start | bytes 294920 | tf_op jit(solution)/shard_map/ppermute | solution.py:179
  4.2 0.8 %collective-permute-done.3 = bf16[384,128]{1,0:T(8,128)(2,1)S(1)} collective-permute-done((bf16[384,128]{1,0:T(8,128)(2,1)S(1)}, bf16[384,128]{1,0:T(8,128)(2,1)S(1)}, u32[]{:S(2)}, u32[]{:S(2)}) %collective-permute-start.3) | collective-permute-done | bytes 98336 | tf_op jit(solution)/shard_map/ppermute | solution.py:179
  5.0 7.9 %collective-permute-done.4 = bf16[384,128]{1,0:T(8,128)(2,1)S(1)} collective-permute-done((bf16[384,128]{1,0:T(8,128)(2,1)S(1)}, bf16[384,128]{1,0:T(8,128)(2,1)S(1)}, u32[]{:S(2)}, u32[]{:S(2)}) %collective-permute-start.4) | collective-permute-done | bytes 98336 | tf_op jit(solution)/shard_map/ppermute | solution.py:179
  12.9 0.0 collective-permute-done.5
  13.0 1.3 %collective-permute-start.11 = (bf16[1152,128]{1,0:T(8,128)(2,1)S(1)}, bf16[1152,128]{1,0:T(8,128)(2,1)S(1)}, u32[]{:S(2)}, u32[]{:S(2)}) collective-permute-start(bf16[1152,128]{1,0:T(8,128)(2,1)S(1)} %constant_dynamic-update-slice_fusion.refs_4_), channel_id=1, source_target_pairs={{0,24},{4,28},{8,16},{12,20},{16,8},{20,12},{24,0},{28,4},{1,25},{... | collective-permute-start | bytes 884744 | tf_op jit(solution)/shard_map/ppermute | solution.py:179
  14.2 0.2 collective-permute-start.9
  14.5 1.2 %collective-permute-start.7 = (bf16[1152,128]{1,0:T(8,128)(2,1)S(1)}, bf16[1152,128]{1,0:T(8,128)(2,1)S(1)}, u32[]{:S(2)}, u32[]{:S(2)}) collective-permute-start(bf16[1152,128]{1,0:T(8,128)(2,1)S(1)} %constant_dynamic-update-slice_fusion.refs_4_), channel_id=1, source_target_pairs={{0,8},{4,12},{8,0},{12,4},{16,24},{20,28},{24,16},{28,20},{1,9},{5... | collective-permute-start | bytes 884744 | tf_op jit(solution)/shard_map/ppermute | solution.py:179
  15.7 1.3 %collective-permute-start.2 = (bf16[384,128]{1,0:T(8,128)(2,1)}, bf16[384,128]{1,0:T(8,128)(2,1)S(1)}, u32[]{:S(2)}, u32[]{:S(2)}) collective-permute-start(bf16[384,128]{1,0:T(8,128)(2,1)} %refs_0_.3), channel_id=1, source_target_pairs={{0,3},{1,2},{2,1},{3,0},{4,7},{5,6},{6,5},{7,4},{8,11},{9,10},{10,... | collective-permute-start | bytes 294920 | tf_op jit(solution)/shard_map/ppermute | solution.py:179
  17.0 0.0 collective-permute-start.1
  17.0 4.3 %collective-permute-done.2.refs_2_.refs_3_ = bf16[384,128]{1,0:T(8,128)(2,1)S(1)} collective-permute-done((bf16[384,128]{1,0:T(8,128)(2,1)}, bf16[384,128]{1,0:T(8,128)(2,1)S(1)}, u32[]{:S(2)}, u32[]{:S(2)}) %collective-permute-start.2) | collective-permute-done | bytes 98336 | tf_op jit(solution)/shard_map/ppermute | solution.py:179
  21.3 0.0 collective-permute-start
  21.3 5.5 %collective-permute-done.1.refs_1_.refs_2_ = bf16[384,128]{1,0:T(8,128)(2,1)S(1)} collective-permute-done((bf16[384,128]{1,0:T(8,128)(2,1)}, bf16[384,128]{1,0:T(8,128)(2,1)S(1)}, u32[]{:S(2)}, u32[]{:S(2)}) %collective-permute-start.1) | collective-permute-done | bytes 98336 | tf_op jit(solution)/shard_map/ppermute | solution.py:179
  26.8 1.0 %collective-permute-start.6 = (bf16[1152,128]{1,0:T(8,128)(2,1)S(1)}, bf16[1152,128]{1,0:T(8,128)(2,1)S(1)}, u32[]{:S(2)}, u32[]{:S(2)}) collective-permute-start(bf16[1152,128]{1,0:T(8,128)(2,1)S(1)} %constant_dynamic-update-slice_fusion.refs_4_), channel_id=1, source_target_pairs={{0,4},{4,0},{8,12},{12,8},{16,20},{20,16},{24,28},{28,24},{1,5},{5... | collective-permute-start | bytes 884744 | tf_op jit(solution)/shard_map/ppermute | solution.py:179
  27.8 0.0 collective-permute-done.11.refs_10_
  27.8 0.0 collective-permute-start.12
  27.8 1.4 %collective-permute-done.9.refs_8_ = bf16[1152,128]{1,0:T(8,128)(2,1)S(1)} collective-permute-done((bf16[1152,128]{1,0:T(8,128)(2,1)S(1)}, bf16[1152,128]{1,0:T(8,128)(2,1)S(1)}, u32[]{:S(2)}, u32[]{:S(2)}) %collective-permute-start.9) | collective-permute-done | bytes 294944 | tf_op jit(solution)/shard_map/ppermute | solution.py:179
  29.2 0.5 collective-permute-start.10
  29.7 0.0 collective-permute-done.7.refs_6_
  29.7 0.1 collective-permute-start.8
  29.8 0.0 copy-start
  29.8 1.1 %copy-done = bf16[384,1024]{1,0:T(8,128)(2,1)S(1)} copy-done((bf16[384,1024]{1,0:T(8,128)(2,1)S(1)}, bf16[384,1024]{1,0:T(8,128)(2,1)}, u32[]{:S(2)}) %copy-start) | copy-done | bytes 786456
  30.9 0.0 copy-start.1
  30.9 1.6 %copy-done.1 = bf16[1024,1024]{1,0:T(8,128)(2,1)S(1)} copy-done((bf16[1024,1024]{1,0:T(8,128)(2,1)S(1)}, bf16[1024,1024]{1,0:T(8,128)(2,1)}, u32[]{:S(2)}) %copy-start.1) | copy-done | bytes 2097176
  32.5 1.6 %copy-done.2 = bf16[1024,1024]{1,0:T(8,128)(2,1)S(1)} copy-done((bf16[1024,1024]{1,0:T(8,128)(2,1)S(1)}, bf16[1024,1024]{1,0:T(8,128)(2,1)}, u32[]{:S(2)}) %copy-start.2) | copy-done | bytes 2097176
  34.1 1.6 %copy-done.4 = bf16[1024,1024]{1,0:T(8,128)(2,1)S(1)} copy-done((bf16[1024,1024]{1,0:T(8,128)(2,1)S(1)}, bf16[1024,1024]{1,0:T(8,128)(2,1)}, u32[]{:S(2)}) %copy-start.4) | copy-done | bytes 2097176
  35.7 0.9 %copy-done.8 = bf16[128,1024]{1,0:T(8,128)(2,1)S(1)} copy-done((bf16[128,1024]{1,0:T(8,128)(2,1)S(1)}, bf16[128,1024]{1,0:T(8,128)(2,1)}, u32[]{:S(2)}) %copy-start.8) | copy-done | bytes 262168
  36.6 0.9 %copy-done.9 = bf16[384,128]{1,0:T(8,128)(2,1)S(1)} copy-done((bf16[384,128]{1,0:T(8,128)(2,1)S(1)}, bf16[384,128]{1,0:T(8,128)(2,1)}, u32[]{:S(2)}) %copy-start.9) | copy-done | bytes 98328
  37.5 0.7 %copy-done.10 = f32[1024]{0:T(1024)S(1)} copy-done((f32[1024]{0:T(1024)S(1)}, f32[1024]{0:T(1024)}, u32[]{:S(2)}) %copy-start.10) | copy-done | bytes 4120
  38.2 0.7 %copy-done.11 = f32[1024]{0:T(1024)S(1)} copy-done((f32[1024]{0:T(1024)S(1)}, f32[1024]{0:T(1024)}, u32[]{:S(2)}) %copy-start.11) | copy-done | bytes 4120
  38.9 0.0 copy-start.12
  38.9 0.0 copy-start.13
  38.9 5.6 %own_block.1 = (f32[384,1024]{1,0:T(8,128)S(1)}, bf16[384,1024]{1,0:T(8,128)(2,1)S(1)}, f32[8,384,256]{2,1,0:T(8,128)S(1)}, f32[8,384,128]{2,1,0:T(8,128)S(1)}) custom-call(bf16[384,128]{1,0:T(8,128)(2,1)S(1)} %copy-done.9, bf16[384,128]{1,0:T(8,128)(2,1)S(1)} %collective-permute-done.1.refs_1_.refs_2_, ...), custom_call_target="tpu_custom_call" | custom-call | flops 6442450944 | bytes 12582912 | tf_op jit(solution)/shard_map/own_block/pallas_call | solution.py:197
  44.5 0.0 collective-permute-done.refs_1_
  44.5 0.0 collective-permute-done.6.refs_5_
  44.5 0.0 collective-permute-done.12.refs_11_
  44.6 0.0 collective-permute-done.10.refs_9_
  44.6 0.0 collective-permute-done.8.refs_7_
  44.6 0.0 copy-done.3
  44.6 0.0 copy-done.5
  44.6 0.0 copy-done.6
  44.6 0.0 copy-done.7
  44.6 0.0 copy-done.12
  44.6 0.0 copy-done.13
  44.6 18.1 %rest_blocks.1 = (f32[384,128]{1,0:T(8,128)}, f32[1,384]{1,0:T(1,128)S(1)}) custom-call(bf16[384,128]{1,0:T(8,128)(2,1)S(1)} %copy-done.9, bf16[384,128]{1,0:T(8,128)(2,1)S(1)} %collective-permute-done.refs_1_, bf16[384,128]{1,0:T(8,128)(2,1)S(1)} %collective-permute-done.1.refs_1_.refs_2_, bf16[384,128]{1,0:T(8,128)(2,1)S(1)} %collective-permute-done.2.refs_2_.refs_3_, ...), custom_call_target="tpu_custom_call" | custom-call | flops 12884901888 | bytes 16777216 | tf_op jit(solution)/shard_map/rest_blocks/pallas_call | solution.py:214
  62.8 0.6 reduce
  (13 shorter events, 0.1 us)
Async XLA Ops:
  1.5 3.5 %collective-permute-start.3 = (bf16[384,128]{1,0:T(8,128)(2,1)S(1)}, bf16[384,128]{1,0:T(8,128)(2,1)S(1)}, u32[]{:S(2)}, u32[]{:S(2)}) collective-permute-start(bf16[384,128]{1,0:T(8,128)(2,1)S(1)} %constant_dynamic-slice_fusion), channel_id=1, source_target_pairs={{0,1},{1,0},{2,3},{3,2},{4,5},{5,4},{6,7},{7,6},{8,9},{9,8},{10,11... | collective-permute-start | bytes 294920 | tf_op jit(solution)/shard_map/ppermute | solution.py:179
  1.7 11.2 %collective-permute-start.5 = (bf16[384,128]{1,0:T(8,128)(2,1)S(1)}, bf16[384,128]{1,0:T(8,128)(2,1)S(1)}, u32[]{:S(2)}, u32[]{:S(2)}) collective-permute-start(bf16[384,128]{1,0:T(8,128)(2,1)S(1)} %constant_dynamic-slice_fusion), channel_id=1, source_target_pairs={{0,3},{1,2},{2,1},{3,0},{4,7},{5,6},{6,5},{7,4},{8,11},{9,10},{10,... | collective-permute-start | bytes 294920 | tf_op jit(solution)/shard_map/ppermute | solution.py:179
  2.8 10.1 %collective-permute-start.4 = (bf16[384,128]{1,0:T(8,128)(2,1)S(1)}, bf16[384,128]{1,0:T(8,128)(2,1)S(1)}, u32[]{:S(2)}, u32[]{:S(2)}) collective-permute-start(bf16[384,128]{1,0:T(8,128)(2,1)S(1)} %constant_dynamic-slice_fusion), channel_id=1, source_target_pairs={{0,2},{1,3},{2,0},{3,1},{4,6},{5,7},{6,4},{7,5},{8,10},{9,11},{10,... | collective-permute-start | bytes 294920 | tf_op jit(solution)/shard_map/ppermute | solution.py:179
  13.0 14.8 %collective-permute-start.11 = (bf16[1152,128]{1,0:T(8,128)(2,1)S(1)}, bf16[1152,128]{1,0:T(8,128)(2,1)S(1)}, u32[]{:S(2)}, u32[]{:S(2)}) collective-permute-start(bf16[1152,128]{1,0:T(8,128)(2,1)S(1)} %constant_dynamic-update-slice_fusion.refs_4_), channel_id=1, source_target_pairs={{0,24},{4,28},{8,16},{12,20},{16,8},{20,12},{24,0},{28,4},{1,25},{... | collective-permute-start | bytes 884744 | tf_op jit(solution)/shard_map/ppermute | solution.py:179
  14.2 14.9 %collective-permute-start.9 = (bf16[1152,128]{1,0:T(8,128)(2,1)S(1)}, bf16[1152,128]{1,0:T(8,128)(2,1)S(1)}, u32[]{:S(2)}, u32[]{:S(2)}) collective-permute-start(bf16[1152,128]{1,0:T(8,128)(2,1)S(1)} %constant_dynamic-update-slice_fusion.refs_4_), channel_id=1, source_target_pairs={{0,16},{4,20},{8,24},{12,28},{16,0},{20,4},{24,8},{28,12},{1,17},{... | collective-permute-start | bytes 884744 | tf_op jit(solution)/shard_map/ppermute | solution.py:179
  14.5 15.2 %collective-permute-start.7 = (bf16[1152,128]{1,0:T(8,128)(2,1)S(1)}, bf16[1152,128]{1,0:T(8,128)(2,1)S(1)}, u32[]{:S(2)}, u32[]{:S(2)}) collective-permute-start(bf16[1152,128]{1,0:T(8,128)(2,1)S(1)} %constant_dynamic-update-slice_fusion.refs_4_), channel_id=1, source_target_pairs={{0,8},{4,12},{8,0},{12,4},{16,24},{20,28},{24,16},{28,20},{1,9},{5... | collective-permute-start | bytes 884744 | tf_op jit(solution)/shard_map/ppermute | solution.py:179
  15.7 5.6 %collective-permute-start.2 = (bf16[384,128]{1,0:T(8,128)(2,1)}, bf16[384,128]{1,0:T(8,128)(2,1)S(1)}, u32[]{:S(2)}, u32[]{:S(2)}) collective-permute-start(bf16[384,128]{1,0:T(8,128)(2,1)} %refs_0_.3), channel_id=1, source_target_pairs={{0,3},{1,2},{2,1},{3,0},{4,7},{5,6},{6,5},{7,4},{8,11},{9,10},{10,... | collective-permute-start | bytes 294920 | tf_op jit(solution)/shard_map/ppermute | solution.py:179
  17.0 9.8 %collective-permute-start.1 = (bf16[384,128]{1,0:T(8,128)(2,1)}, bf16[384,128]{1,0:T(8,128)(2,1)S(1)}, u32[]{:S(2)}, u32[]{:S(2)}) collective-permute-start(bf16[384,128]{1,0:T(8,128)(2,1)} %refs_0_.3), channel_id=1, source_target_pairs={{0,2},{1,3},{2,0},{3,1},{4,6},{5,7},{6,4},{7,5},{8,10},{9,11},{10,... | collective-permute-start | bytes 294920 | tf_op jit(solution)/shard_map/ppermute | solution.py:179
  21.3 23.3 %collective-permute-start = (bf16[384,128]{1,0:T(8,128)(2,1)}, bf16[384,128]{1,0:T(8,128)(2,1)S(1)}, u32[]{:S(2)}, u32[]{:S(2)}) collective-permute-start(bf16[384,128]{1,0:T(8,128)(2,1)} %refs_0_.3), channel_id=1, source_target_pairs={{0,1},{1,0},{2,3},{3,2},{4,5},{5,4},{6,7},{7,6},{8,9},{9,8},{10,11... | collective-permute-start | bytes 294920 | tf_op jit(solution)/shard_map/ppermute | solution.py:179
  26.8 17.8 %collective-permute-start.6 = (bf16[1152,128]{1,0:T(8,128)(2,1)S(1)}, bf16[1152,128]{1,0:T(8,128)(2,1)S(1)}, u32[]{:S(2)}, u32[]{:S(2)}) collective-permute-start(bf16[1152,128]{1,0:T(8,128)(2,1)S(1)} %constant_dynamic-update-slice_fusion.refs_4_), channel_id=1, source_target_pairs={{0,4},{4,0},{8,12},{12,8},{16,20},{20,16},{24,28},{28,24},{1,5},{5... | collective-permute-start | bytes 884744 | tf_op jit(solution)/shard_map/ppermute | solution.py:179
  27.8 16.7 %collective-permute-start.12 = (bf16[1152,128]{1,0:T(8,128)(2,1)S(1)}, bf16[1152,128]{1,0:T(8,128)(2,1)S(1)}, u32[]{:S(2)}, u32[]{:S(2)}) collective-permute-start(bf16[1152,128]{1,0:T(8,128)(2,1)S(1)} %collective-permute-done.11.refs_10_), channel_id=1, source_target_pairs={{0,4},{4,0},{8,12},{12,8},{16,20},{20,16},{24,28},{28,24},{1,5},{5... | collective-permute-start | bytes 884744 | tf_op jit(solution)/shard_map/ppermute | solution.py:179
  29.2 15.4 %collective-permute-start.10 = (bf16[1152,128]{1,0:T(8,128)(2,1)S(1)}, bf16[1152,128]{1,0:T(8,128)(2,1)S(1)}, u32[]{:S(2)}, u32[]{:S(2)}) collective-permute-start(bf16[1152,128]{1,0:T(8,128)(2,1)S(1)} %collective-permute-done.9.refs_8_), channel_id=1, source_target_pairs={{0,4},{4,0},{8,12},{12,8},{16,20},{20,16},{24,28},{28,24},{1,5},{5... | collective-permute-start | bytes 884744 | tf_op jit(solution)/shard_map/ppermute | solution.py:179
  29.7 14.9 %collective-permute-start.8 = (bf16[1152,128]{1,0:T(8,128)(2,1)S(1)}, bf16[1152,128]{1,0:T(8,128)(2,1)S(1)}, u32[]{:S(2)}, u32[]{:S(2)}) collective-permute-start(bf16[1152,128]{1,0:T(8,128)(2,1)S(1)} %collective-permute-done.7.refs_6_), channel_id=1, source_target_pairs={{0,4},{4,0},{8,12},{12,8},{16,20},{20,16},{24,28},{28,24},{1,5},{5... | collective-permute-start | bytes 884744 | tf_op jit(solution)/shard_map/ppermute | solution.py:179
  29.8 1.1 %copy-start = (bf16[384,1024]{1,0:T(8,128)(2,1)S(1)}, bf16[384,1024]{1,0:T(8,128)(2,1)}, u32[]{:S(2)}) copy-start(bf16[384,1024]{1,0:T(8,128)(2,1)} %refs_3_.1) | copy-start | bytes 2359300
  30.9 1.6 %copy-start.1 = (bf16[1024,1024]{1,0:T(8,128)(2,1)S(1)}, bf16[1024,1024]{1,0:T(8,128)(2,1)}, u32[]{:S(2)}) copy-start(bf16[1024,1024]{1,0:T(8,128)(2,1)} %refs_7_.1) | copy-start | bytes 6291460
  32.5 1.6 %copy-start.2 = (bf16[1024,1024]{1,0:T(8,128)(2,1)S(1)}, bf16[1024,1024]{1,0:T(8,128)(2,1)}, u32[]{:S(2)}) copy-start(bf16[1024,1024]{1,0:T(8,128)(2,1)} %refs_19_.1) | copy-start | bytes 6291460
  34.1 1.6 %copy-start.4 = (bf16[1024,1024]{1,0:T(8,128)(2,1)S(1)}, bf16[1024,1024]{1,0:T(8,128)(2,1)}, u32[]{:S(2)}) copy-start(bf16[1024,1024]{1,0:T(8,128)(2,1)} %refs_20_.1) | copy-start | bytes 6291460
  35.7 0.9 %copy-start.8 = (bf16[128,1024]{1,0:T(8,128)(2,1)S(1)}, bf16[128,1024]{1,0:T(8,128)(2,1)}, u32[]{:S(2)}) copy-start(bf16[128,1024]{1,0:T(8,128)(2,1)} %refs_16_.1) | copy-start | bytes 786436
  36.6 0.9 %copy-start.9 = (bf16[384,128]{1,0:T(8,128)(2,1)S(1)}, bf16[384,128]{1,0:T(8,128)(2,1)}, u32[]{:S(2)}) copy-start(bf16[384,128]{1,0:T(8,128)(2,1)} %refs_0_.3) | copy-start | bytes 294916
  37.5 0.7 %copy-start.10 = (f32[1024]{0:T(1024)S(1)}, f32[1024]{0:T(1024)}, u32[]{:S(2)}) copy-start(f32[1024]{0:T(1024)} %param.15) | copy-start | bytes 12292
  38.2 0.7 %copy-start.11 = (f32[1024]{0:T(1024)S(1)}, f32[1024]{0:T(1024)}, u32[]{:S(2)}) copy-start(f32[1024]{0:T(1024)} %param.16) | copy-start | bytes 12292
  38.9 5.7 %copy-start.3 = (bf16[1024,1024]{1,0:T(8,128)(2,1)S(1)}, bf16[1024,1024]{1,0:T(8,128)(2,1)}, u32[]{:S(2)}) copy-start(bf16[1024,1024]{1,0:T(8,128)(2,1)} %refs_19_.1) | copy-start | bytes 6291460
  38.9 5.7 %copy-start.5 = (bf16[1024,1024]{1,0:T(8,128)(2,1)S(1)}, bf16[1024,1024]{1,0:T(8,128)(2,1)}, u32[]{:S(2)}) copy-start(bf16[1024,1024]{1,0:T(8,128)(2,1)} %refs_20_.1) | copy-start | bytes 6291460
  38.9 5.7 %copy-start.6 = (bf16[1024,1024]{1,0:T(8,128)(2,1)S(1)}, bf16[1024,1024]{1,0:T(8,128)(2,1)}, u32[]{:S(2)}) copy-start(bf16[1024,1024]{1,0:T(8,128)(2,1)} %refs_21_.1) | copy-start | bytes 6291460
  38.9 5.7 %copy-start.7 = (bf16[1024,256]{1,0:T(8,128)(2,1)S(1)}, bf16[1024,256]{1,0:T(8,128)(2,1)}, u32[]{:S(2)}) copy-start(bf16[1024,256]{1,0:T(8,128)(2,1)} %refs_23_.1) | copy-start | bytes 1572868
  38.9 5.7 %copy-start.12 = (f32[1024]{0:T(1024)S(1)}, f32[1024]{0:T(1024)}, u32[]{:S(2)}) copy-start(f32[1024]{0:T(1024)} %param.21) | copy-start | bytes 12292
  38.9 5.7 %copy-start.13 = (f32[256]{0:T(256)S(1)}, f32[256]{0:T(256)}, u32[]{:S(2)}) copy-start(f32[256]{0:T(256)} %param.23) | copy-start | bytes 3076

commit v2 on v1

v2 whole, which is shorter than its diff:
```python
import functools
import math

import jax
import jax.numpy as jnp
from jax import lax
from jax.experimental import pallas as pl
from jax.experimental.pallas import tpu as pltpu
from jax.sharding import PartitionSpec as P

H = 8
LANES = 128
PAD = 16
F32 = jnp.float32
BF16 = jnp.bfloat16
VMEM = pltpu.VMEM
HBM = pltpu.HBM


def dot(a, b):
    return jnp.dot(a, b, preferred_element_type=F32)


def normalize(values, gain):
    mean = jnp.mean(values, axis=-1, keepdims=True)
    centred = values - mean
    spread = jnp.mean(centred * centred, axis=-1, keepdims=True)
    return centred * lax.rsqrt(spread + 1e-05) * gain


def place_patches(slots, refs, held, rows, me):
    if slots is None:
        held[: held.shape[0] - PAD] = refs[0][...]
    else:
        for slot, ref in zip(slots, refs):
            start = pl.multiple_of(jnp.bitwise_xor(me, slot) * rows, rows)
            held[pl.ds(start, rows)] = ref[...]
    held[held.shape[0] - PAD :] = jnp.zeros((PAD, held.shape[1]), BF16)


def window(held, block, rows, count):
    start = pl.multiple_of((count - 1 - block) * rows, rows)
    return held[pl.ds(start, rows + PAD)]


def reverse(part, last):
    rows = part.shape[0] - PAD
    row = lax.broadcasted_iota(jnp.int32, (rows, rows + PAD), 0)
    col = lax.broadcasted_iota(jnp.int32, (rows, rows + PAD), 1)
    return dot((row + col == last).astype(BF16), part)


def from_patches(part, w_in, b_in):
    rows = part.shape[0] - PAD
    return dot(reverse(part, rows).astype(BF16), w_in) + b_in


def scores_of(queries, keys):
    return lax.dot_general(queries, keys, (((1,), (1,)), ((), ())), preferred_element_type=F32)


def repeat(column, width):
    return jnp.concatenate([column] * (width // LANES), axis=1)


def with_ones(values):
    return jnp.concatenate([values, jnp.ones((values.shape[0], LANES), BF16)], axis=1)


def load_kernel(n, *refs):
    sems = refs[2 * n]
    moves = [pltpu.make_async_copy(refs[i], refs[n + i], sems.at[i]) for i in range(n)]
    for move in moves:
        move.start()
    for move in moves:
        move.wait()


def own_kernel(slots, places, count, n_patch, *refs):
    patch_refs = refs[:n_patch]
    (pos, w_in, b_in, gain, w_query, w_key, w_value) = refs[n_patch : n_patch + 7]
    (hidden_out, query_out, acc_out, top_out, parts_out, flipped_out, held) = refs[n_patch + 7 :]
    rows = pos.shape[0]
    head = w_query.shape[1] // H
    me = lax.axis_index("seq")
    place_patches(slots, patch_refs, held, rows, me)
    own = window(held, me, rows, count)
    flipped_out[...] = reverse(own, rows - 1)
    hidden = from_patches(own, w_in[...], b_in[...]) + pos[...].astype(F32)
    hidden_out[...] = hidden
    normed = normalize(hidden, gain[...]).astype(BF16)
    scale = math.log2(math.e) / math.sqrt(head)
    query_out[...] = (dot(normed, w_query[...]) * scale).astype(BF16)
    keys = dot(normed, w_key[...]).astype(BF16)
    values = dot(normed, w_value[...]).astype(BF16)
    row = lax.broadcasted_iota(jnp.int32, (rows, rows), 0)
    col = lax.broadcasted_iota(jnp.int32, (rows, rows), 1)
    allowed = col <= row
    ahead = scores_of(query_out[:, :head], keys[:, :head])
    for h in range(H):
        scores = jnp.where(allowed, ahead, -1e30)
        if h + 1 < H:
            part = slice((h + 1) * head, (h + 2) * head)
            ahead = scores_of(query_out[:, part], keys[:, part])
        top = jnp.broadcast_to(jnp.max(scores, axis=1, keepdims=True), (rows, LANES))
        weights = jnp.exp2(scores - repeat(top, rows)).astype(BF16)
        top_out[h] = top
        acc_out[h] = dot(weights, with_ones(values[:, h * head : (h + 1) * head]))
    if slots is None:

        def step(block, carry):
            parts_out[block] = from_patches(window(held, block, rows, count), w_in[...], b_in[...])
            return carry

        lax.fori_loop(0, me, step, 0)
    else:
        for i, place in enumerate(places):
            block = jnp.bitwise_xor(me, place)
            parts_out[i] = from_patches(window(held, block, rows, count), w_in[...], b_in[...])


def add_block(query, hid, gain, w_key, w_value, acc, top, bias):
    rows = query.shape[0]
    head = query.shape[1] // H
    normed = normalize(hid, gain[...]).astype(BF16)
    keys = dot(normed, w_key[...]).astype(BF16)
    values = dot(normed, w_value[...]).astype(BF16)
    ahead = scores_of(query[:, :head], keys[:, :head])
    for h in range(H):
        scores = ahead
        if h + 1 < H:
            part = slice((h + 1) * head, (h + 2) * head)
            ahead = scores_of(query[:, part], keys[:, part])
        old = top[h]
        new = jnp.maximum(old, jnp.max(scores, axis=1, keepdims=True) - bias)
        weights = jnp.exp2(scores - repeat(new + bias, rows)).astype(BF16)
        factor = jnp.exp2(old - new)
        top[h] = new
        acc[h] = acc[h] * repeat(factor, head + LANES) + dot(weights, with_ones(values[:, h * head : (h + 1) * head]))


def place_positions(mine, other, pos_held):
    group = lax.axis_index("dp")
    for i in range(mine.shape[0]):
        pos_held[jnp.bitwise_xor(group, 2 * i)] = mine[i]
        pos_held[jnp.bitwise_xor(group, 2 * i + 1)] = other[i]


def rest_kernel(places, n_pos, *refs):
    (hidden, query, _, _, parts, flipped) = refs[:6]
    pos_refs = refs[6 : n_pos + 6]
    weights = refs[n_pos + 6 : n_pos + 9]
    (w_proj, out_gain, w_out, b_out) = refs[n_pos + 9 : n_pos + 13]
    (latent_out, logdet_out, acc, top) = refs[n_pos + 13 : n_pos + 17]
    rows, width = hidden.shape
    head = width // H
    feats = flipped.shape[1]
    me = lax.axis_index("seq")
    if places is None:

        def step(block, carry):
            add_block(query, parts[block] + pos_refs[0][block].astype(F32), *weights, acc, top, 0.0)
            return carry

        lax.fori_loop(0, me, step, 0)
    else:
        pos_held = refs[-1]
        place_positions(*pos_refs, pos_held)
        for i, place in enumerate(places):
            bias = jnp.where(jnp.bitwise_xor(me, place) < me, 0.0, 1e30).astype(F32)
            pos = [pos_held[c, i * rows : (i + 1) * rows] for c in range(pos_held.shape[0])]
            hid = parts[i] + jnp.concatenate(pos, axis=1).astype(F32)
            add_block(query, hid, *weights, acc, top, bias)
    attended = jnp.concatenate([(acc[h][:, :head] / acc[h][:, head:]).astype(BF16) for h in range(H)], axis=1)
    mixed = hidden[...] + dot(attended, w_proj[...])
    second = normalize(mixed, out_gain[...]).astype(BF16)
    stats = dot(second, w_out[...]) + b_out[...]
    shift_part = stats[:, :feats]
    log_scale = stats[:, feats:]
    latent_out[...] = (flipped[...] - shift_part) * jnp.exp(-log_scale)
    logdet_out[...] = -jnp.mean(jnp.transpose(log_scale), axis=0)


def spec(n, memory=VMEM):
    return [pl.BlockSpec(memory_space=memory)] * n


def stay(array):
    return pltpu.with_memory_space_constraint(array, HBM)


def cost(flops):
    return pl.CostEstimate(flops=flops, bytes_accessed=1 << 20, transcendentals=0)


def shards(
    patches, pos_embed, w_in, b_in, ln_gain, w_query, w_key, w_value, w_proj, out_gain, w_out, b_out
):
    count = lax.axis_size("seq")
    groups = lax.axis_size("dp")
    rows, feats = patches.shape
    width = w_query.shape[0]
    head = width // H
    b_in, ln_gain, out_gain, b_out = [a.reshape(1, -1) for a in (b_in, ln_gain, out_gain, b_out)]
    quick = count == 4 and groups == 8 and width == groups * LANES
    if quick:
        group = lax.axis_index("dp")
        cut = lax.dynamic_slice_in_dim(pos_embed, group * LANES, LANES, 1)

        def swap(block, axis, mask, size):
            return lax.ppermute(block, axis, [(i, i ^ mask) for i in range(size)])

        def send(block, pairs):
            return lax.ppermute(block, "seq", pairs)

        along = [
            send(cut, [(2, 3), (0, 1)]),
            send(cut, [(1, 3), (0, 2)]),
            send(cut, [(0, 3), (1, 2)]),
        ]
        after = lax.optimization_barrier((patches, cut))[0]
        patch_list = [
            patches,
            send(after, [(2, 3), (3, 2)]),
            send(after, [(1, 3), (3, 1)]),
            send(after, [(0, 3), (1, 2), (2, 1), (3, 0)]),
        ]
        slots = (0, 1, 2, 3)
        places = (1, 2, 3)
    else:
        slots = places = None
        patch_list = [lax.all_gather(patches, "seq", axis=0, tiled=True)]
        pos_list = [lax.all_gather(pos_embed, "seq", axis=0, tiled=False)]
    own_given = (pos_embed, w_in, b_in, ln_gain, w_query, w_key, w_value)
    if quick:
        own_given = pl.pallas_call(
            functools.partial(load_kernel, len(own_given)),
            out_shape=[VMEM(a.shape, a.dtype) for a in own_given],
            in_specs=spec(len(own_given), HBM),
            out_specs=spec(len(own_given)),
            scratch_shapes=[pltpu.SemaphoreType.DMA((len(own_given),))],
            compiler_params=pltpu.CompilerParams(vmem_limit_bytes=1 << 20),
            cost_estimate=cost(1),
            name="load_weights",
        )(*[stay(a) for a in own_given])
        own_given = list(own_given)
        *along, own_given[1] = lax.optimization_barrier((*along, own_given[1]))
        *patch_list[1:], own_given[1] = lax.optimization_barrier((*patch_list[1:], own_given[1]))
        mine = jnp.concatenate(along, axis=0)
        plane = [mine] + [swap(mine, "dp", m, groups) for m in (2, 4, 6)]
    (_, w_in, b_in, ln_gain, _, w_key, w_value) = own_given
    state = (
        jax.ShapeDtypeStruct((H, rows, head + LANES), F32),
        jax.ShapeDtypeStruct((H, rows, LANES), F32),
    )
    n = len(patch_list)
    hidden, query, acc, top, parts, flipped = pl.pallas_call(
        functools.partial(own_kernel, slots, places, count, n),
        out_shape=(
            jax.ShapeDtypeStruct((rows, width), F32),
            jax.ShapeDtypeStruct((rows, width), BF16),
            *state,
            jax.ShapeDtypeStruct((count - 1, rows, width), F32),
            jax.ShapeDtypeStruct((rows, feats), F32),
        ),
        in_specs=spec(n + 7),
        out_specs=spec(6),
        scratch_shapes=[VMEM((count * rows + PAD, feats), BF16)],
        compiler_params=pltpu.CompilerParams(vmem_limit_bytes=(16 if quick else 52) << 20),
        cost_estimate=cost(1),
        name="own_block",
    )(*patch_list, *own_given)
    if quick:
        query, *plane = lax.optimization_barrier((query, *plane))
        plane = jnp.stack(plane)
        pos_list = (plane, swap(plane, "dp", 1, groups))
    n = len(pos_list)
    latent, logdet, _, _ = pl.pallas_call(
        functools.partial(rest_kernel, places, n),
        out_shape=(jax.ShapeDtypeStruct((rows, feats), F32), jax.ShapeDtypeStruct((rows,), F32)) + state,
        in_specs=spec(n + 13),
        out_specs=spec(4),
        scratch_shapes=[VMEM((groups, (count - 1) * rows, LANES), BF16)] if quick else [],
        input_output_aliases={2: 2, 3: 3},
        compiler_params=pltpu.CompilerParams(vmem_limit_bytes=(20 if quick else 60) << 20),
        cost_estimate=cost(1),
        name="other_blocks",
    )(hidden, query, acc, top, parts, flipped, *pos_list, ln_gain, w_key, w_value, w_proj, out_gain, w_out, b_out)
    return (latent, logdet)


def solution(mesh):
    in_specs = (
        P(("dp", "seq"), None),
        P("seq", None),
        P(),
        P(),
        P(),
        P(),
        P(),
        P(),
        P(),
        P(),
        P(),
        P(),
    )
    out_specs = (P(("dp", "seq"), None), P(("dp", "seq")))
    return jax.shard_map(shards, mesh=mesh, in_specs=in_specs, out_specs=out_specs, check_vma=False)
```

time: 63.8 us -> 56.6 us (0.89)
  local copies, waits for them, and re-layouts: 10.1 us -> 0.97 us
  starting transfers between devices: 8.3 us -> 13.9 us
  waiting for transfers between devices: 19.9 us -> 15.2 us
  Pallas kernels: 23.7 us -> 25.4 us
    ppermute x13 -> x4, waiting for transfers between devices: 19.9 us -> 2.48 us  [swap(): return lax.ppermute(block, axis, [(i, i ^ mask) for i in range(size)])]
    ppermute x0 -> x6, waiting for transfers between devices: none -> 12.7 us  [send(): return lax.ppermute(block, 'seq', pairs)]
    unnamed x30 -> x12, local copies, waits for them, and re-layouts: 9.17 us -> 0.05 us
    ppermute x0 -> x6, starting transfers between devices: none -> 7.69 us  [send(): return lax.ppermute(block, 'seq', pairs)]
    ppermute x13 -> x4, starting transfers between devices: 8.3 us -> 6.25 us  [swap(): return lax.ppermute(block, axis, [(i, i ^ mask) for i in range(size)])]
    pallas_call x2 -> x3, Pallas kernels: 23.7 us -> 25.4 us  [the longest x1 15.7 us: shards(): pl.pallas_call(functools.partial(rest_kernel, places, n), out_shape=(jax....]
  transfers between devices with their start and end apart: 13 -> 10, of which waited for: 5 -> 6; matrix products, arithmetic and copies ran while one was open for 0% -> 0% of each run, Pallas kernels for 9% -> 17%
where the time goes in v2:
time: 56.6 us; the launch traced here: 56.4 us
  Pallas kernels  25.4 us (45%)
  waiting for transfers between devices  15.2 us (27%)
  starting transfers between devices  13.9 us (25%)
  local copies, waits for them, and re-layouts  0.97 us (2%)
  between operations  0.78 us (1%)
    pallas_call x1, Pallas kernels, shards(): pl.pallas_call(functools.partial(rest_kernel, places, n), out_shape=(jax....  15.7 us
    ppermute x6, waiting for transfers between devices, send(): return lax.ppermute(block, 'seq', pairs)  12.7 us
    ppermute x6, starting transfers between devices, send(): return lax.ppermute(block, 'seq', pairs)  7.69 us
    pallas_call x1, Pallas kernels, shards(): pl.pallas_call(functools.partial(own_kernel, slots, places, count, n), ou...  6.32 us
    ppermute x4, starting transfers between devices, swap(): return lax.ppermute(block, axis, [(i, i ^ mask) for i in range(size)])  6.25 us
    pallas_call x1, Pallas kernels, shards(): pl.pallas_call(functools.partial(load_kernel, len(own_given)), out_shape=...  3.31 us
    ppermute x4, waiting for transfers between devices, swap(): return lax.ppermute(block, axis, [(i, i ^ mask) for i in range(size)])  2.48 us
  transfers between devices with their start and end apart: 10, of which 6 were waited for; matrix products, arithmetic and copies ran while one was open for 0% of the time, Pallas kernels for 17%

profile of v2, /device:TPU:27, one launch (start us, length us, event | category | flops | bytes accessed | tf_op | source)
XLA Modules:
  0.0 56.4 jit_solution(7786604884789250298)
XLA Ops:
  0.6 0.9 %constant_dynamic-slice_fusion = bf16[384,128]{1,0:T(8,128)(2,1)S(1)} fusion(bf16[384,1024]{1,0:T(8,128)(2,1)} %refs_0_.2, s32[]{:T(128)S(6)} %select_n.3), kind=kLoop, calls=%fused_computation.4 | loop fusion | bytes 196612 | tf_op jit(solution)/shard_map/dynamic_slice | solution.py:208
  1.5 1.3 %collective-permute-start.5 = (bf16[384,128]{1,0:T(8,128)(2,1)S(1)}, bf16[384,128]{1,0:T(8,128)(2,1)S(1)}, u32[]{:S(2)}, u32[]{:S(2)}) collective-permute-start(bf16[384,128]{1,0:T(8,128)(2,1)S(1)} %constant_dynamic-slice_fusion), channel_id=1, source_target_pairs={{0,3},{1,2},{4,7},{5,6},{8,11},{9,10},{12,15},{13,14},{16,19},{17,... | collective-permute-start | bytes 294920 | tf_op jit(solution)/shard_map/ppermute | solution.py:214
  2.8 1.3 %collective-permute-start.4 = (bf16[384,128]{1,0:T(8,128)(2,1)S(1)}, bf16[384,128]{1,0:T(8,128)(2,1)S(1)}, u32[]{:S(2)}, u32[]{:S(2)}) collective-permute-start(bf16[384,128]{1,0:T(8,128)(2,1)S(1)} %constant_dynamic-slice_fusion), channel_id=1, source_target_pairs={{1,3},{0,2},{5,7},{4,6},{9,11},{8,10},{13,15},{12,14},{17,19},{16,... | collective-permute-start | bytes 294920 | tf_op jit(solution)/shard_map/ppermute | solution.py:214
  4.1 1.3 %collective-permute-start.3 = (bf16[384,128]{1,0:T(8,128)(2,1)S(1)}, bf16[384,128]{1,0:T(8,128)(2,1)S(1)}, u32[]{:S(2)}, u32[]{:S(2)}) collective-permute-start(bf16[384,128]{1,0:T(8,128)(2,1)S(1)} %constant_dynamic-slice_fusion), channel_id=1, source_target_pairs={{2,3},{0,1},{6,7},{4,5},{10,11},{8,9},{14,15},{12,13},{18,19},{16,... | collective-permute-start | bytes 294920 | tf_op jit(solution)/shard_map/ppermute | solution.py:214
  5.4 0.0 copy-start.2
  5.4 3.3 %load_weights.1 = (bf16[384,1024]{1,0:T(8,128)(2,1)S(1)}, bf16[128,1024]{1,0:T(8,128)(2,1)S(1)}, f32[1,1024]{1,0:T(1,128)S(1)}, f32[1,1024]{1,0:T(1,128)S(1)}, b...) custom-call(bf16[384,1024]{1,0:T(8,128)(2,1)} %refs_0_.2, ...), custom_call_target="tpu_custom_call" | custom-call | flops 1 | bytes 1048576 | tf_op jit(solution)/shard_map/load_weights/pallas_call | solution.py:236
  8.8 0.1 collective-permute-done.5
  8.8 5.5 %collective-permute-done.4 = bf16[384,128]{1,0:T(8,128)(2,1)S(1)} collective-permute-done((bf16[384,128]{1,0:T(8,128)(2,1)S(1)}, bf16[384,128]{1,0:T(8,128)(2,1)S(1)}, u32[]{:S(2)}, u32[]{:S(2)}) %collective-permute-start.4) | collective-permute-done | bytes 98336 | tf_op jit(solution)/shard_map/ppermute | solution.py:214
  14.4 0.0 collective-permute-done.3
  14.4 1.3 %collective-permute-start.8 = (bf16[1152,128]{1,0:T(8,128)(2,1)S(1)}, bf16[1152,128]{1,0:T(8,128)(2,1)S(1)}, u32[]{:S(2)}, u32[]{:S(2)}) collective-permute-start(bf16[1152,128]{1,0:T(8,128)(2,1)S(1)} %constant_dynamic-update-slice_fusion), channel_id=1, source_target_pairs={{0,24},{4,28},{8,16},{12,20},{16,8},{20,12},{24,0},{28,4},{1,25},{... | collective-permute-start | bytes 884744 | tf_op jit(solution)/shard_map/ppermute | solution.py:211
  15.7 0.2 collective-permute-start.7
  15.9 1.2 %collective-permute-start.6 = (bf16[1152,128]{1,0:T(8,128)(2,1)S(1)}, bf16[1152,128]{1,0:T(8,128)(2,1)S(1)}, u32[]{:S(2)}, u32[]{:S(2)}) collective-permute-start(bf16[1152,128]{1,0:T(8,128)(2,1)S(1)} %constant_dynamic-update-slice_fusion), channel_id=1, source_target_pairs={{0,8},{4,12},{8,0},{12,4},{16,24},{20,28},{24,16},{28,20},{1,9},{5... | collective-permute-start | bytes 884744 | tf_op jit(solution)/shard_map/ppermute | solution.py:211
  17.1 0.0 copy-done.2
  17.1 0.0 collective-permute-start.2
  17.1 1.9 %collective-permute-start.1 = (bf16[384,128]{1,0:T(8,128)(2,1)S(1)}, bf16[384,128]{1,0:T(8,128)(2,1)S(1)}, u32[]{:S(2)}, u32[]{:S(2)}) collective-permute-start(bf16[384,128]{1,0:T(8,128)(2,1)S(1)} %copy-done.2), channel_id=1, source_target_pairs={{1,3},{3,1},{5,7},{7,5},{9,11},{11,9},{13,15},{15,13},{17,19},{19,... | collective-permute-start | bytes 294920 | tf_op jit(solution)/shard_map/ppermute | solution.py:214
  19.1 3.4 %collective-permute-done.2.refs_3_ = bf16[384,128]{1,0:T(8,128)(2,1)S(1)} collective-permute-done((bf16[384,128]{1,0:T(8,128)(2,1)S(1)}, bf16[384,128]{1,0:T(8,128)(2,1)S(1)}, u32[]{:S(2)}, u32[]{:S(2)}) %collective-permute-start.2) | collective-permute-done | bytes 98336 | tf_op jit(solution)/shard_map/ppermute | solution.py:214
  22.4 1.9 %collective-permute-start = (bf16[384,128]{1,0:T(8,128)(2,1)S(1)}, bf16[384,128]{1,0:T(8,128)(2,1)S(1)}, u32[]{:S(2)}, u32[]{:S(2)}) collective-permute-start(bf16[384,128]{1,0:T(8,128)(2,1)S(1)} %copy-done.2), channel_id=1, source_target_pairs={{2,3},{3,2},{6,7},{7,6},{10,11},{11,10},{14,15},{15,14},{18,19},{1... | collective-permute-start | bytes 294920 | tf_op jit(solution)/shard_map/ppermute | solution.py:214
  24.3 0.6 %collective-permute-done.1.refs_2_ = bf16[384,128]{1,0:T(8,128)(2,1)S(1)} collective-permute-done((bf16[384,128]{1,0:T(8,128)(2,1)S(1)}, bf16[384,128]{1,0:T(8,128)(2,1)S(1)}, u32[]{:S(2)}, u32[]{:S(2)}) %collective-permute-start.1) | collective-permute-done | bytes 98336 | tf_op jit(solution)/shard_map/ppermute | solution.py:214
  24.9 3.2 %collective-permute-done.refs_1_ = bf16[384,128]{1,0:T(8,128)(2,1)S(1)} collective-permute-done((bf16[384,128]{1,0:T(8,128)(2,1)S(1)}, bf16[384,128]{1,0:T(8,128)(2,1)S(1)}, u32[]{:S(2)}, u32[]{:S(2)}) %collective-permute-start) | collective-permute-done | bytes 98336 | tf_op jit(solution)/shard_map/ppermute | solution.py:214
  28.1 0.0 copy-start.1
  28.1 6.3 %own_block.1 = (f32[384,1024]{1,0:T(8,128)S(1)}, bf16[384,1024]{1,0:T(8,128)(2,1)S(1)}, f32[8,384,256]{2,1,0:T(8,128)S(1)}, f32[8,384,128]{2,1,0:T(8,128)S(1)}, ...) custom-call(bf16[384,128]{1,0:T(8,128)(2,1)S(1)} %copy-done.2, bf16[384,128]{1,0:T(8,128)(2,1)S(1)} %collective-permute-done.refs_1_, ...), custom_call_target="tpu_custom_call" | custom-call | flops 1 | bytes 1048576 | tf_op jit(solution)/shard_map/own_block/pallas_call | solution.py:257
  34.4 0.0 copy-start
  34.4 0.0 copy-start.3
  34.4 0.0 copy-start.4
  34.4 0.0 collective-permute-done.8
  34.4 0.0 collective-permute-done.7
  34.4 0.0 collective-permute-done.6
  34.5 0.2 pad_maximum_fusion.refs_6_
  34.6 3.5 %collective-permute-start.9 = (bf16[4,1152,128]{2,1,0:T(8,128)(2,1)S(1)}, bf16[4,1152,128]{2,1,0:T(8,128)(2,1)S(1)}, u32[]{:S(2)}, u32[]{:S(2)}) collective-permute-start(bf16[4,1152,128]{2,1,0:T(8,128)(2,1)S(1)} %pad_maximum_fusion.refs_6_), channel_id=1, source_target_pairs={{0,4},{4,0},{8,12},{12,8},{16,20},{20,16},{24,28},{28,24},{1,5},{5... | collective-permute-start | bytes 3538952 | tf_op jit(solution)/shard_map/ppermute | solution.py:211
  38.2 2.5 %collective-permute-done.9.refs_7_ = bf16[4,1152,128]{2,1,0:T(8,128)(2,1)S(1)} collective-permute-done((bf16[4,1152,128]{2,1,0:T(8,128)(2,1)S(1)}, bf16[4,1152,128]{2,1,0:T(8,128)(2,1)S(1)}, u32[]{:S(2)}, u32[]{:S(2)}) %collective-permute-start.9) | collective-permute-done | bytes 1179680 | tf_op jit(solution)/shard_map/ppermute | solution.py:211
  40.6 0.0 copy-done.1
  40.6 0.0 copy-done
  40.6 0.0 copy-done.3
  40.6 0.0 copy-done.4
  40.6 15.7 %other_blocks.1 = (f32[384,128]{1,0:T(8,128)}, f32[384]{0:T(512)}, f32[8,384,256]{2,1,0:T(8,128)S(1)}, f32[8,384,128]{2,1,0:T(8,128)S(1)}) custom-call(f32[384,1024]{1,0:T(8,128)S(1)} %get-tuple-element.44.refs_0_, bf16[384,1024]{1,0:T(8,128)(2,1)S(1)} %get-tuple-element.49.refs_1_, ...), custom_call_target="tpu_custom_call", output_to_operand_aliasing={{2}: (2, {}), {3}: (3, {})} | custom-call | flops 1 | bytes 1048576 | tf_op jit(solution)/shard_map/other_blocks/pallas_call | solution.py:278
  (3 shorter events, 0.0 us)
Async XLA Ops:
  1.5 7.3 %collective-permute-start.5 = (bf16[384,128]{1,0:T(8,128)(2,1)S(1)}, bf16[384,128]{1,0:T(8,128)(2,1)S(1)}, u32[]{:S(2)}, u32[]{:S(2)}) collective-permute-start(bf16[384,128]{1,0:T(8,128)(2,1)S(1)} %constant_dynamic-slice_fusion), channel_id=1, source_target_pairs={{0,3},{1,2},{4,7},{5,6},{8,11},{9,10},{12,15},{13,14},{16,19},{17,... | collective-permute-start | bytes 294920 | tf_op jit(solution)/shard_map/ppermute | solution.py:214
  2.8 11.5 %collective-permute-start.4 = (bf16[384,128]{1,0:T(8,128)(2,1)S(1)}, bf16[384,128]{1,0:T(8,128)(2,1)S(1)}, u32[]{:S(2)}, u32[]{:S(2)}) collective-permute-start(bf16[384,128]{1,0:T(8,128)(2,1)S(1)} %constant_dynamic-slice_fusion), channel_id=1, source_target_pairs={{1,3},{0,2},{5,7},{4,6},{9,11},{8,10},{13,15},{12,14},{17,19},{16,... | collective-permute-start | bytes 294920 | tf_op jit(solution)/shard_map/ppermute | solution.py:214
  4.1 10.2 %collective-permute-start.3 = (bf16[384,128]{1,0:T(8,128)(2,1)S(1)}, bf16[384,128]{1,0:T(8,128)(2,1)S(1)}, u32[]{:S(2)}, u32[]{:S(2)}) collective-permute-start(bf16[384,128]{1,0:T(8,128)(2,1)S(1)} %constant_dynamic-slice_fusion), channel_id=1, source_target_pairs={{2,3},{0,1},{6,7},{4,5},{10,11},{8,9},{14,15},{12,13},{18,19},{16,... | collective-permute-start | bytes 294920 | tf_op jit(solution)/shard_map/ppermute | solution.py:214
  5.4 11.7 %copy-start.2 = (bf16[384,128]{1,0:T(8,128)(2,1)S(1)}, bf16[384,128]{1,0:T(8,128)(2,1)}, u32[]{:S(2)}) copy-start(bf16[384,128]{1,0:T(8,128)(2,1)} %refs_0_.3) | copy-start | bytes 294916
  14.4 20.0 %collective-permute-start.8 = (bf16[1152,128]{1,0:T(8,128)(2,1)S(1)}, bf16[1152,128]{1,0:T(8,128)(2,1)S(1)}, u32[]{:S(2)}, u32[]{:S(2)}) collective-permute-start(bf16[1152,128]{1,0:T(8,128)(2,1)S(1)} %constant_dynamic-update-slice_fusion), channel_id=1, source_target_pairs={{0,24},{4,28},{8,16},{12,20},{16,8},{20,12},{24,0},{28,4},{1,25},{... | collective-permute-start | bytes 884744 | tf_op jit(solution)/shard_map/ppermute | solution.py:211
  15.7 18.7 %collective-permute-start.7 = (bf16[1152,128]{1,0:T(8,128)(2,1)S(1)}, bf16[1152,128]{1,0:T(8,128)(2,1)S(1)}, u32[]{:S(2)}, u32[]{:S(2)}) collective-permute-start(bf16[1152,128]{1,0:T(8,128)(2,1)S(1)} %constant_dynamic-update-slice_fusion), channel_id=1, source_target_pairs={{0,16},{4,20},{8,24},{12,28},{16,0},{20,4},{24,8},{28,12},{1,17},{... | collective-permute-start | bytes 884744 | tf_op jit(solution)/shard_map/ppermute | solution.py:211
  15.9 18.5 %collective-permute-start.6 = (bf16[1152,128]{1,0:T(8,128)(2,1)S(1)}, bf16[1152,128]{1,0:T(8,128)(2,1)S(1)}, u32[]{:S(2)}, u32[]{:S(2)}) collective-permute-start(bf16[1152,128]{1,0:T(8,128)(2,1)S(1)} %constant_dynamic-update-slice_fusion), channel_id=1, source_target_pairs={{0,8},{4,12},{8,0},{12,4},{16,24},{20,28},{24,16},{28,20},{1,9},{5... | collective-permute-start | bytes 884744 | tf_op jit(solution)/shard_map/ppermute | solution.py:211
  17.1 5.3 %collective-permute-start.2 = (bf16[384,128]{1,0:T(8,128)(2,1)S(1)}, bf16[384,128]{1,0:T(8,128)(2,1)S(1)}, u32[]{:S(2)}, u32[]{:S(2)}) collective-permute-start(bf16[384,128]{1,0:T(8,128)(2,1)S(1)} %copy-done.2), channel_id=1, source_target_pairs={{0,3},{1,2},{2,1},{3,0},{4,7},{5,6},{6,5},{7,4},{8,11},{9,10},{10,... | collective-permute-start | bytes 294920 | tf_op jit(solution)/shard_map/ppermute | solution.py:214
  17.1 7.8 %collective-permute-start.1 = (bf16[384,128]{1,0:T(8,128)(2,1)S(1)}, bf16[384,128]{1,0:T(8,128)(2,1)S(1)}, u32[]{:S(2)}, u32[]{:S(2)}) collective-permute-start(bf16[384,128]{1,0:T(8,128)(2,1)S(1)} %copy-done.2), channel_id=1, source_target_pairs={{1,3},{3,1},{5,7},{7,5},{9,11},{11,9},{13,15},{15,13},{17,19},{19,... | collective-permute-start | bytes 294920 | tf_op jit(solution)/shard_map/ppermute | solution.py:214
  22.4 5.6 %collective-permute-start = (bf16[384,128]{1,0:T(8,128)(2,1)S(1)}, bf16[384,128]{1,0:T(8,128)(2,1)S(1)}, u32[]{:S(2)}, u32[]{:S(2)}) collective-permute-start(bf16[384,128]{1,0:T(8,128)(2,1)S(1)} %copy-done.2), channel_id=1, source_target_pairs={{2,3},{3,2},{6,7},{7,6},{10,11},{11,10},{14,15},{15,14},{18,19},{1... | collective-permute-start | bytes 294920 | tf_op jit(solution)/shard_map/ppermute | solution.py:214
  28.1 12.6 %copy-start.1 = (bf16[1024,256]{1,0:T(8,128)(2,1)S(1)}, bf16[1024,256]{1,0:T(8,128)(2,1)}, u32[]{:S(2)}) copy-start(bf16[1024,256]{1,0:T(8,128)(2,1)} %refs_13_.1) | copy-start | bytes 1572868
  34.4 6.2 %copy-start = (bf16[1024,1024]{1,0:T(8,128)(2,1)S(1)}, bf16[1024,1024]{1,0:T(8,128)(2,1)}, u32[]{:S(2)}) copy-start(bf16[1024,1024]{1,0:T(8,128)(2,1)} %refs_11_.1) | copy-start | bytes 6291460
  34.4 6.2 %copy-start.3 = (f32[1024]{0:T(1024)S(1)}, f32[1024]{0:T(1024)}, u32[]{:S(2)}) copy-start(f32[1024]{0:T(1024)} %param.21) | copy-start | bytes 12292
  34.4 6.2 %copy-start.4 = (f32[256]{0:T(256)S(1)}, f32[256]{0:T(256)}, u32[]{:S(2)}) copy-start(f32[256]{0:T(256)} %param.23) | copy-start | bytes 3076
  34.6 6.0 %collective-permute-start.9 = (bf16[4,1152,128]{2,1,0:T(8,128)(2,1)S(1)}, bf16[4,1152,128]{2,1,0:T(8,128)(2,1)S(1)}, u32[]{:S(2)}, u32[]{:S(2)}) collective-permute-start(bf16[4,1152,128]{2,1,0:T(8,128)(2,1)S(1)} %pad_maximum_fusion.refs_6_), channel_id=1, source_target_pairs={{0,4},{4,0},{8,12},{12,8},{16,20},{20,16},{24,28},{28,24},{1,5},{5... | collective-permute-start | bytes 3538952 | tf_op jit(solution)/shard_map/ppermute | solution.py:211

commit v3 on v2

--- a/solution.py
+++ b/solution.py
@@ -78,20 +78,39 @@
 
 def own_kernel(slots, places, count, n_patch, *refs):
     patch_refs = refs[:n_patch]
-    (pos, w_in, b_in, gain, w_query, w_key, w_value) = refs[n_patch : n_patch + 7]
-    (hidden_out, query_out, acc_out, top_out, parts_out, flipped_out, held) = refs[n_patch + 7 :]
+    (w_in, b_in, pos, gain) = refs[n_patch : n_patch + 4]
+    given = refs[n_patch + 4 : n_patch + 7]
+    (hidden_out, query_out, acc_out, top_out, parts_out, flipped_out, w_key, w_value) = refs[n_patch + 7 : n_patch + 15]
+    (held, w_query, sems) = refs[n_patch + 15 :]
+    moves = [pltpu.make_async_copy(a, b, sems.at[i]) for i, (a, b) in enumerate(zip(given, (w_query, w_key, w_value)))]
+    for move in moves:
+        move.start()
     rows = pos.shape[0]
     head = w_query.shape[1] // H
     me = lax.axis_index("seq")
     place_patches(slots, patch_refs, held, rows, me)
+    if slots is None:
+
+        def step(block, carry):
+            parts_out[block] = from_patches(window(held, block, rows, count), w_in[...], b_in[...])
+            return carry
+
+        lax.fori_loop(0, me, step, 0)
+    else:
+        for i, place in enumerate(places):
+            block = jnp.bitwise_xor(me, place)
+            parts_out[i] = from_patches(window(held, block, rows, count), w_in[...], b_in[...])
     own = window(held, me, rows, count)
     flipped_out[...] = reverse(own, rows - 1)
     hidden = from_patches(own, w_in[...], b_in[...]) + pos[...].astype(F32)
     hidden_out[...] = hidden
     normed = normalize(hidden, gain[...]).astype(BF16)
     scale = math.log2(math.e) / math.sqrt(head)
+    moves[0].wait()
     query_out[...] = (dot(normed, w_query[...]) * scale).astype(BF16)
+    moves[1].wait()
     keys = dot(normed, w_key[...]).astype(BF16)
+    moves[2].wait()
     values = dot(normed, w_value[...]).astype(BF16)
     row = lax.broadcasted_iota(jnp.int32, (rows, rows), 0)
     col = lax.broadcasted_iota(jnp.int32, (rows, rows), 1)
@@ -106,36 +125,50 @@
         weights = jnp.exp2(scores - repeat(top, rows)).astype(BF16)
         top_out[h] = top
         acc_out[h] = dot(weights, with_ones(values[:, h * head : (h + 1) * head]))
-    if slots is None:
-
-        def step(block, carry):
-            parts_out[block] = from_patches(window(held, block, rows, count), w_in[...], b_in[...])
-            return carry
-
-        lax.fori_loop(0, me, step, 0)
-    else:
-        for i, place in enumerate(places):
-            block = jnp.bitwise_xor(me, place)
-            parts_out[i] = from_patches(window(held, block, rows, count), w_in[...], b_in[...])
-
-
-def add_block(query, hid, gain, w_key, w_value, acc, top, bias):
+
+
+def add_block(query, hid, gain, w_key, w_value, acc, top):
     rows = query.shape[0]
     head = query.shape[1] // H
     normed = normalize(hid, gain[...]).astype(BF16)
     keys = dot(normed, w_key[...]).astype(BF16)
     values = dot(normed, w_value[...]).astype(BF16)
+    for h in range(H):
+        part = slice(h * head, (h + 1) * head)
+        scores = scores_of(query[:, part], keys[:, part])
+        old = top[h]
+        new = jnp.maximum(old, jnp.max(scores, axis=1, keepdims=True))
+        weights = jnp.exp2(scores - repeat(new, rows)).astype(BF16)
+        factor = jnp.exp2(old - new)
+        top[h] = new
+        acc[h] = acc[h] * repeat(factor, head + LANES) + dot(weights, with_ones(values[:, part]))
+
+
+def add_blocks(query, places, parts, pos_held, gain, w_key, w_value, normed, keys, values, acc, top):
+    rows = query.shape[0]
+    head = query.shape[1] // H
+    me = lax.axis_index("seq")
+    biases, spans = [], []
+    for i, place in enumerate(places):
+        biases.append(jnp.where(jnp.bitwise_xor(me, place) < me, 0.0, 1e30).astype(F32))
+        span = slice(i * rows, (i + 1) * rows)
+        spans.append(span)
+        pos = jnp.concatenate([pos_held[c, span] for c in range(pos_held.shape[0])], axis=1)
+        normed[span] = normalize(parts[i] + pos.astype(F32), gain[...]).astype(BF16)
+        keys[span] = dot(normed[span], w_key[...]).astype(BF16)
+        values[span] = dot(normed[span], w_value[...]).astype(BF16)
     ahead = scores_of(query[:, :head], keys[:, :head])
     for h in range(H):
         scores = ahead
         if h + 1 < H:
             part = slice((h + 1) * head, (h + 2) * head)
             ahead = scores_of(query[:, part], keys[:, part])
-        old = top[h]
-        new = jnp.maximum(old, jnp.max(scores, axis=1, keepdims=True) - bias)
-        weights = jnp.exp2(scores - repeat(new + bias, rows)).astype(BF16)
+        old = new = top[h]
+        for span, bias in zip(spans, biases):
+            new = jnp.maximum(new, jnp.max(scores[:, span], axis=1, keepdims=True) - bias)
+        pieces = [jnp.exp2(scores[:, span] - repeat(new + bias, rows)).astype(BF16) for span, bias in zip(spans, biases)]
         factor = jnp.exp2(old - new)
-        top[h] = new
+        weights = jnp.concatenate(pieces, axis=1)
         acc[h] = acc[h] * repeat(factor, head + LANES) + dot(weights, with_ones(values[:, h * head : (h + 1) * head]))
 
 
@@ -159,18 +192,14 @@
     if places is None:
 
         def step(block, carry):
-            add_block(query, parts[block] + pos_refs[0][block].astype(F32), *weights, acc, top, 0.0)
+            add_block(query, parts[block] + pos_refs[0][block].astype(F32), *weights, acc, top)
             return carry
 
         lax.fori_loop(0, me, step, 0)
     else:
-        pos_held = refs[-1]
+        (pos_held, normed, keys, values) = refs[n_pos + 17 :]
         place_positions(*pos_refs, pos_held)
-        for i, place in enumerate(places):
-            bias = jnp.where(jnp.bitwise_xor(me, place) < me, 0.0, 1e30).astype(F32)
-            pos = [pos_held[c, i * rows : (i + 1) * rows] for c in range(pos_held.shape[0])]
-            hid = parts[i] + jnp.concatenate(pos, axis=1).astype(F32)
-            add_block(query, hid, *weights, acc, top, bias)
+        add_blocks(query, places, parts, pos_held, *weights, normed, keys, values, acc, top)
     attended = jnp.concatenate([(acc[h][:, :head] / acc[h][:, head:]).astype(BF16) for h in range(H)], axis=1)
     mixed = hidden[...] + dot(attended, w_proj[...])
     second = normalize(mixed, out_gain[...]).astype(BF16)
@@ -231,7 +260,7 @@
         slots = places = None
         patch_list = [lax.all_gather(patches, "seq", axis=0, tiled=True)]
         pos_list = [lax.all_gather(pos_embed, "seq", axis=0, tiled=False)]
-    own_given = (pos_embed, w_in, b_in, ln_gain, w_query, w_key, w_value)
+    own_given = (w_in, b_in, pos_embed, ln_gain)
     if quick:
         own_given = pl.pallas_call(
             functools.partial(load_kernel, len(own_given)),
@@ -248,28 +277,32 @@
         *patch_list[1:], own_given[1] = lax.optimization_barrier((*patch_list[1:], own_given[1]))
         mine = jnp.concatenate(along, axis=0)
         plane = [mine] + [swap(mine, "dp", m, groups) for m in (2, 4, 6)]
-    (_, w_in, b_in, ln_gain, _, w_key, w_value) = own_given
-    state = (
-        jax.ShapeDtypeStruct((H, rows, head + LANES), F32),
-        jax.ShapeDtypeStruct((H, rows, LANES), F32),
-    )
+        ln_gain = own_given[3]
+    here = VMEM if quick else jax.ShapeDtypeStruct
+    state = (here((H, rows, head + LANES), F32), here((H, rows, LANES), F32))
     n = len(patch_list)
-    hidden, query, acc, top, parts, flipped = pl.pallas_call(
+    hidden, query, acc, top, parts, flipped, w_key, w_value = pl.pallas_call(
         functools.partial(own_kernel, slots, places, count, n),
         out_shape=(
-            jax.ShapeDtypeStruct((rows, width), F32),
-            jax.ShapeDtypeStruct((rows, width), BF16),
+            here((rows, width), F32),
+            here((rows, width), BF16),
             *state,
-            jax.ShapeDtypeStruct((count - 1, rows, width), F32),
-            jax.ShapeDtypeStruct((rows, feats), F32),
+            here((count - 1, rows, width), F32),
+            here((rows, feats), F32),
+            here(w_key.shape, BF16),
+            here(w_value.shape, BF16),
         ),
-        in_specs=spec(n + 7),
-        out_specs=spec(6),
-        scratch_shapes=[VMEM((count * rows + PAD, feats), BF16)],
-        compiler_params=pltpu.CompilerParams(vmem_limit_bytes=(16 if quick else 52) << 20),
-        cost_estimate=cost(1),
+        in_specs=spec(n + 4) + spec(3, HBM),
+        out_specs=spec(8),
+        scratch_shapes=[
+            VMEM((count * rows + PAD, feats), BF16),
+            VMEM(w_query.shape, BF16),
+            pltpu.SemaphoreType.DMA((3,)),
+        ],
+        compiler_params=pltpu.CompilerParams(vmem_limit_bytes=(20 if quick else 54) << 20),
+        cost_estimate=cost(1 << 36),
         name="own_block",
-    )(*patch_list, *own_given)
+    )(*patch_list, *own_given, *[stay(a) for a in (w_query, w_key, w_value)])
     if quick:
         query, *plane = lax.optimization_barrier((query, *plane))
         plane = jnp.stack(plane)
@@ -280,7 +313,9 @@
         out_shape=(jax.ShapeDtypeStruct((rows, feats), F32), jax.ShapeDtypeStruct((rows,), F32)) + state,
         in_specs=spec(n + 13),
         out_specs=spec(4),
-        scratch_shapes=[VMEM((groups, (count - 1) * rows, LANES), BF16)] if quick else [],
+        scratch_shapes=[VMEM((groups, (count - 1) * rows, LANES), BF16)] + [VMEM(((count - 1) * rows, width), BF16)] * 3
+        if quick
+        else [],
         input_output_aliases={2: 2, 3: 3},
         compiler_params=pltpu.CompilerParams(vmem_limit_bytes=(20 if quick else 60) << 20),
         cost_estimate=cost(1),

time: 56.6 us -> 50.6 us (0.89)
  the two profiles are of different devices: /device:TPU:27 before, /device:TPU:19 now
where the time goes in v3:
time: 50.6 us; the launch traced here: 50.3 us
  Pallas kernels  23.6 us (47%)
  starting transfers between devices  16.8 us (33%)
  waiting for transfers between devices  7.97 us (16%)
  local copies, waits for them, and re-layouts  1 us (2%)
  between operations  0.79 us (2%)
    pallas_call x1, Pallas kernels, shards(): pl.pallas_call(functools.partial(rest_kernel, places, n), out_shape=(jax....  14 us
    ppermute x6, starting transfers between devices, send(): return lax.ppermute(block, 'seq', pairs)  13.8 us
    pallas_call x1, Pallas kernels, shards(): pl.pallas_call(functools.partial(own_kernel, slots, places, count, n), ou...  8.35 us
    ppermute x4, waiting for transfers between devices, swap(): return lax.ppermute(block, axis, [(i, i ^ mask) for i in range(size)])  5.95 us
    ppermute x4, starting transfers between devices, swap(): return lax.ppermute(block, axis, [(i, i ^ mask) for i in range(size)])  2.97 us
    ppermute x6, waiting for transfers between devices, send(): return lax.ppermute(block, 'seq', pairs)  2.02 us
    pallas_call x1, Pallas kernels, shards(): pl.pallas_call(functools.partial(load_kernel, len(own_given)), out_shape=...  1.28 us
  transfers between devices with their start and end apart: 10, of which 4 were waited for; matrix products, arithmetic and copies ran while one was open for 0% of the time, Pallas kernels for 19%

profile of v3, /device:TPU:19, one launch (start us, length us, event | category | flops | bytes accessed | tf_op | source)
XLA Modules:
  0.0 50.3 jit_solution(15091056290036976643)
XLA Ops:
  0.6 0.0 copy-start.4
  0.6 0.9 %constant_dynamic-slice_fusion = bf16[384,128]{1,0:T(8,128)(2,1)S(1)} fusion(bf16[384,1024]{1,0:T(8,128)(2,1)} %refs_2_.1, s32[]{:T(128)S(6)} %select_n.3), kind=kLoop, calls=%fused_computation.4 | loop fusion | bytes 196612 | tf_op jit(solution)/shard_map/dynamic_slice | solution.py:237
  1.6 1.3 %collective-permute-start.5 = (bf16[384,128]{1,0:T(8,128)(2,1)S(1)}, bf16[384,128]{1,0:T(8,128)(2,1)S(1)}, u32[]{:S(2)}, u32[]{:S(2)}) collective-permute-start(bf16[384,128]{1,0:T(8,128)(2,1)S(1)} %constant_dynamic-slice_fusion), channel_id=1, source_target_pairs={{0,3},{1,2},{4,7},{5,6},{8,11},{9,10},{12,15},{13,14},{16,19},{17,... | collective-permute-start | bytes 294920 | tf_op jit(solution)/shard_map/ppermute | solution.py:243
  2.9 1.3 %collective-permute-start.4 = (bf16[384,128]{1,0:T(8,128)(2,1)S(1)}, bf16[384,128]{1,0:T(8,128)(2,1)S(1)}, u32[]{:S(2)}, u32[]{:S(2)}) collective-permute-start(bf16[384,128]{1,0:T(8,128)(2,1)S(1)} %constant_dynamic-slice_fusion), channel_id=1, source_target_pairs={{1,3},{0,2},{5,7},{4,6},{9,11},{8,10},{13,15},{12,14},{17,19},{16,... | collective-permute-start | bytes 294920 | tf_op jit(solution)/shard_map/ppermute | solution.py:243
  4.2 3.2 %collective-permute-start.3 = (bf16[384,128]{1,0:T(8,128)(2,1)S(1)}, bf16[384,128]{1,0:T(8,128)(2,1)S(1)}, u32[]{:S(2)}, u32[]{:S(2)}) collective-permute-start(bf16[384,128]{1,0:T(8,128)(2,1)S(1)} %constant_dynamic-slice_fusion), channel_id=1, source_target_pairs={{2,3},{0,1},{6,7},{4,5},{10,11},{8,9},{14,15},{12,13},{18,19},{16,... | collective-permute-start | bytes 294920 | tf_op jit(solution)/shard_map/ppermute | solution.py:243
  7.4 1.2 %collective-permute-start.2 = (bf16[384,128]{1,0:T(8,128)(2,1)}, bf16[384,128]{1,0:T(8,128)(2,1)S(1)}, u32[]{:S(2)}, u32[]{:S(2)}) collective-permute-start(bf16[384,128]{1,0:T(8,128)(2,1)} %refs_0_.3), channel_id=1, source_target_pairs={{0,3},{1,2},{2,1},{3,0},{4,7},{5,6},{6,5},{7,4},{8,11},{9,10},{10,... | collective-permute-start | bytes 294920 | tf_op jit(solution)/shard_map/ppermute | solution.py:243
  8.6 0.7 %collective-permute-start.1 = (bf16[384,128]{1,0:T(8,128)(2,1)}, bf16[384,128]{1,0:T(8,128)(2,1)S(1)}, u32[]{:S(2)}, u32[]{:S(2)}) collective-permute-start(bf16[384,128]{1,0:T(8,128)(2,1)} %refs_0_.3), channel_id=1, source_target_pairs={{1,3},{3,1},{5,7},{7,5},{9,11},{11,9},{13,15},{15,13},{17,19},{19,... | collective-permute-start | bytes 294920 | tf_op jit(solution)/shard_map/ppermute | solution.py:243
  9.3 1.3 %load_weights.1 = (bf16[128,1024]{1,0:T(8,128)(2,1)S(1)}, f32[1,1024]{1,0:T(1,128)S(1)}, bf16[384,1024]{1,0:T(8,128)(2,1)S(1)}, f32[1,1024]{1,0:T(1,128)S(1)}) custom-call(bf16[128,1024]{1,0:T(8,128)(2,1)} %refs_0_.2, f32[1,1024]{1,0:T(1,128)} %bitcast.14, bf16[384,1024]{1,0:T(8,128)(2,1)} %refs_2_.1, f32[1,1024]{1,0:T(1,128)} %bitcast.15), custom_call_target="tpu_custom_call" | custom-call | flops 1 | bytes 1048576 | tf_op jit(solution)/shard_map/load_weights/pallas_call | solution.py:265
  10.6 0.0 collective-permute-done.5
  10.6 6.1 %collective-permute-start = (bf16[384,128]{1,0:T(8,128)(2,1)}, bf16[384,128]{1,0:T(8,128)(2,1)S(1)}, u32[]{:S(2)}, u32[]{:S(2)}) collective-permute-start(bf16[384,128]{1,0:T(8,128)(2,1)} %refs_0_.3), channel_id=1, source_target_pairs={{2,3},{3,2},{6,7},{7,6},{10,11},{11,10},{14,15},{15,14},{18,19},{1... | collective-permute-start | bytes 294920 | tf_op jit(solution)/shard_map/ppermute | solution.py:243
  16.7 0.0 collective-permute-done.4
  16.8 0.0 collective-permute-done.3
  16.8 1.3 %collective-permute-start.8 = (bf16[1152,128]{1,0:T(8,128)(2,1)S(1)}, bf16[1152,128]{1,0:T(8,128)(2,1)S(1)}, u32[]{:S(2)}, u32[]{:S(2)}) collective-permute-start(bf16[1152,128]{1,0:T(8,128)(2,1)S(1)} %constant_dynamic-update-slice_fusion), channel_id=1, source_target_pairs={{0,24},{4,28},{8,16},{12,20},{16,8},{20,12},{24,0},{28,4},{1,25},{... | collective-permute-start | bytes 884744 | tf_op jit(solution)/shard_map/ppermute | solution.py:240
  18.1 0.2 collective-permute-start.7
  18.3 0.4 collective-permute-done.2.refs_3_
  18.7 0.8 %collective-permute-start.6 = (bf16[1152,128]{1,0:T(8,128)(2,1)S(1)}, bf16[1152,128]{1,0:T(8,128)(2,1)S(1)}, u32[]{:S(2)}, u32[]{:S(2)}) collective-permute-start(bf16[1152,128]{1,0:T(8,128)(2,1)S(1)} %constant_dynamic-update-slice_fusion), channel_id=1, source_target_pairs={{0,8},{4,12},{8,0},{12,4},{16,24},{20,28},{24,16},{28,20},{1,9},{5... | collective-permute-start | bytes 884744 | tf_op jit(solution)/shard_map/ppermute | solution.py:240
  19.5 0.0 collective-permute-done.1.refs_2_
  19.6 1.6 %collective-permute-done.refs_1_ = bf16[384,128]{1,0:T(8,128)(2,1)S(1)} collective-permute-done((bf16[384,128]{1,0:T(8,128)(2,1)}, bf16[384,128]{1,0:T(8,128)(2,1)S(1)}, u32[]{:S(2)}, u32[]{:S(2)}) %collective-permute-start) | collective-permute-done | bytes 98336 | tf_op jit(solution)/shard_map/ppermute | solution.py:243
  21.2 0.0 copy-done.4
  21.2 0.0 copy-start.1
  21.2 8.4 %own_block.1 = (f32[384,1024]{1,0:T(8,128)S(1)}, bf16[384,1024]{1,0:T(8,128)(2,1)S(1)}, f32[8,384,256]{2,1,0:T(8,128)S(1)}, f32[8,384,128]{2,1,0:T(8,128)S(1)}, ...) custom-call(bf16[384,128]{1,0:T(8,128)(2,1)S(1)} %copy-done.4, ...), custom_call_target="tpu_custom_call" | custom-call | flops 68719476736 | bytes 1048576 | tf_op jit(solution)/shard_map/own_block/pallas_call | solution.py:284
  29.5 0.0 copy-start
  29.5 0.0 copy-start.2
  29.5 0.0 copy-start.3
  29.6 0.0 collective-permute-done.8
  29.6 3.5 %collective-permute-done.7 = bf16[1152,128]{1,0:T(8,128)(2,1)S(1)} collective-permute-done((bf16[1152,128]{1,0:T(8,128)(2,1)S(1)}, bf16[1152,128]{1,0:T(8,128)(2,1)S(1)}, u32[]{:S(2)}, u32[]{:S(2)}) %collective-permute-start.7) | collective-permute-done | bytes 294944 | tf_op jit(solution)/shard_map/ppermute | solution.py:240
  33.0 0.0 collective-permute-done.6
  33.0 0.1 pad_maximum_fusion.refs_6_
  33.2 0.7 %collective-permute-start.9 = (bf16[4,1152,128]{2,1,0:T(8,128)(2,1)S(1)}, bf16[4,1152,128]{2,1,0:T(8,128)(2,1)S(1)}, u32[]{:S(2)}, u32[]{:S(2)}) collective-permute-start(bf16[4,1152,128]{2,1,0:T(8,128)(2,1)S(1)} %pad_maximum_fusion.refs_6_), channel_id=1, source_target_pairs={{0,4},{4,0},{8,12},{12,8},{16,20},{20,16},{24,28},{28,24},{1,5},{5... | collective-permute-start | bytes 3538952 | tf_op jit(solution)/shard_map/ppermute | solution.py:240
  33.9 2.5 %collective-permute-done.9.refs_7_ = bf16[4,1152,128]{2,1,0:T(8,128)(2,1)S(1)} collective-permute-done((bf16[4,1152,128]{2,1,0:T(8,128)(2,1)S(1)}, bf16[4,1152,128]{2,1,0:T(8,128)(2,1)S(1)}, u32[]{:S(2)}, u32[]{:S(2)}) %collective-permute-start.9) | collective-permute-done | bytes 1179680 | tf_op jit(solution)/shard_map/ppermute | solution.py:240
  36.3 0.0 copy-done.1
  36.3 0.0 copy-done
  36.3 0.0 copy-done.2
  36.3 0.0 copy-done.3
  36.3 14.0 %other_blocks.1 = (f32[384,128]{1,0:T(8,128)}, f32[384]{0:T(512)}, f32[8,384,256]{2,1,0:T(8,128)S(1)}, f32[8,384,128]{2,1,0:T(8,128)S(1)}) custom-call(f32[384,1024]{1,0:T(8,128)S(1)} %get-tuple-element.40.refs_0_, bf16[384,1024]{1,0:T(8,128)(2,1)S(1)} %get-tuple-element.45.refs_1_, ...), custom_call_target="tpu_custom_call", output_to_operand_aliasing={{2}: (2, {}), {3}: (3, {})} | custom-call | flops 1 | bytes 1048576 | tf_op jit(solution)/shard_map/other_blocks/pallas_call | solution.py:311
  (3 shorter events, 0.0 us)
Async XLA Ops:
  0.6 20.5 %copy-start.4 = (bf16[384,128]{1,0:T(8,128)(2,1)S(1)}, bf16[384,128]{1,0:T(8,128)(2,1)}, u32[]{:S(2)}) copy-start(bf16[384,128]{1,0:T(8,128)(2,1)} %refs_0_.3) | copy-start | bytes 294916
  1.6 9.0 %collective-permute-start.5 = (bf16[384,128]{1,0:T(8,128)(2,1)S(1)}, bf16[384,128]{1,0:T(8,128)(2,1)S(1)}, u32[]{:S(2)}, u32[]{:S(2)}) collective-permute-start(bf16[384,128]{1,0:T(8,128)(2,1)S(1)} %constant_dynamic-slice_fusion), channel_id=1, source_target_pairs={{0,3},{1,2},{4,7},{5,6},{8,11},{9,10},{12,15},{13,14},{16,19},{17,... | collective-permute-start | bytes 294920 | tf_op jit(solution)/shard_map/ppermute | solution.py:243
  2.9 13.9 %collective-permute-start.4 = (bf16[384,128]{1,0:T(8,128)(2,1)S(1)}, bf16[384,128]{1,0:T(8,128)(2,1)S(1)}, u32[]{:S(2)}, u32[]{:S(2)}) collective-permute-start(bf16[384,128]{1,0:T(8,128)(2,1)S(1)} %constant_dynamic-slice_fusion), channel_id=1, source_target_pairs={{1,3},{0,2},{5,7},{4,6},{9,11},{8,10},{13,15},{12,14},{17,19},{16,... | collective-permute-start | bytes 294920 | tf_op jit(solution)/shard_map/ppermute | solution.py:243
  4.2 12.6 %collective-permute-start.3 = (bf16[384,128]{1,0:T(8,128)(2,1)S(1)}, bf16[384,128]{1,0:T(8,128)(2,1)S(1)}, u32[]{:S(2)}, u32[]{:S(2)}) collective-permute-start(bf16[384,128]{1,0:T(8,128)(2,1)S(1)} %constant_dynamic-slice_fusion), channel_id=1, source_target_pairs={{2,3},{0,1},{6,7},{4,5},{10,11},{8,9},{14,15},{12,13},{18,19},{16,... | collective-permute-start | bytes 294920 | tf_op jit(solution)/shard_map/ppermute | solution.py:243
  7.4 11.4 %collective-permute-start.2 = (bf16[384,128]{1,0:T(8,128)(2,1)}, bf16[384,128]{1,0:T(8,128)(2,1)S(1)}, u32[]{:S(2)}, u32[]{:S(2)}) collective-permute-start(bf16[384,128]{1,0:T(8,128)(2,1)} %refs_0_.3), channel_id=1, source_target_pairs={{0,3},{1,2},{2,1},{3,0},{4,7},{5,6},{6,5},{7,4},{8,11},{9,10},{10,... | collective-permute-start | bytes 294920 | tf_op jit(solution)/shard_map/ppermute | solution.py:243
  8.6 10.9 %collective-permute-start.1 = (bf16[384,128]{1,0:T(8,128)(2,1)}, bf16[384,128]{1,0:T(8,128)(2,1)S(1)}, u32[]{:S(2)}, u32[]{:S(2)}) collective-permute-start(bf16[384,128]{1,0:T(8,128)(2,1)} %refs_0_.3), channel_id=1, source_target_pairs={{1,3},{3,1},{5,7},{7,5},{9,11},{11,9},{13,15},{15,13},{17,19},{19,... | collective-permute-start | bytes 294920 | tf_op jit(solution)/shard_map/ppermute | solution.py:243
  10.6 10.6 %collective-permute-start = (bf16[384,128]{1,0:T(8,128)(2,1)}, bf16[384,128]{1,0:T(8,128)(2,1)S(1)}, u32[]{:S(2)}, u32[]{:S(2)}) collective-permute-start(bf16[384,128]{1,0:T(8,128)(2,1)} %refs_0_.3), channel_id=1, source_target_pairs={{2,3},{3,2},{6,7},{7,6},{10,11},{11,10},{14,15},{15,14},{18,19},{1... | collective-permute-start | bytes 294920 | tf_op jit(solution)/shard_map/ppermute | solution.py:243
  16.8 12.7 %collective-permute-start.8 = (bf16[1152,128]{1,0:T(8,128)(2,1)S(1)}, bf16[1152,128]{1,0:T(8,128)(2,1)S(1)}, u32[]{:S(2)}, u32[]{:S(2)}) collective-permute-start(bf16[1152,128]{1,0:T(8,128)(2,1)S(1)} %constant_dynamic-update-slice_fusion), channel_id=1, source_target_pairs={{0,24},{4,28},{8,16},{12,20},{16,8},{20,12},{24,0},{28,4},{1,25},{... | collective-permute-start | bytes 884744 | tf_op jit(solution)/shard_map/ppermute | solution.py:240
  18.1 14.9 %collective-permute-start.7 = (bf16[1152,128]{1,0:T(8,128)(2,1)S(1)}, bf16[1152,128]{1,0:T(8,128)(2,1)S(1)}, u32[]{:S(2)}, u32[]{:S(2)}) collective-permute-start(bf16[1152,128]{1,0:T(8,128)(2,1)S(1)} %constant_dynamic-update-slice_fusion), channel_id=1, source_target_pairs={{0,16},{4,20},{8,24},{12,28},{16,0},{20,4},{24,8},{28,12},{1,17},{... | collective-permute-start | bytes 884744 | tf_op jit(solution)/shard_map/ppermute | solution.py:240
  18.7 14.3 %collective-permute-start.6 = (bf16[1152,128]{1,0:T(8,128)(2,1)S(1)}, bf16[1152,128]{1,0:T(8,128)(2,1)S(1)}, u32[]{:S(2)}, u32[]{:S(2)}) collective-permute-start(bf16[1152,128]{1,0:T(8,128)(2,1)S(1)} %constant_dynamic-update-slice_fusion), channel_id=1, source_target_pairs={{0,8},{4,12},{8,0},{12,4},{16,24},{20,28},{24,16},{28,20},{1,9},{5... | collective-permute-start | bytes 884744 | tf_op jit(solution)/shard_map/ppermute | solution.py:240
  21.2 15.2 %copy-start.1 = (bf16[1024,256]{1,0:T(8,128)(2,1)S(1)}, bf16[1024,256]{1,0:T(8,128)(2,1)}, u32[]{:S(2)}) copy-start(bf16[1024,256]{1,0:T(8,128)(2,1)} %refs_13_.1) | copy-start | bytes 1572868
  29.5 6.8 %copy-start = (bf16[1024,1024]{1,0:T(8,128)(2,1)S(1)}, bf16[1024,1024]{1,0:T(8,128)(2,1)}, u32[]{:S(2)}) copy-start(bf16[1024,1024]{1,0:T(8,128)(2,1)} %refs_11_.1) | copy-start | bytes 6291460
  29.5 6.8 %copy-start.2 = (f32[1024]{0:T(1024)S(1)}, f32[1024]{0:T(1024)}, u32[]{:S(2)}) copy-start(f32[1024]{0:T(1024)} %param.21) | copy-start | bytes 12292
  29.5 6.8 %copy-start.3 = (f32[256]{0:T(256)S(1)}, f32[256]{0:T(256)}, u32[]{:S(2)}) copy-start(f32[256]{0:T(256)} %param.23) | copy-start | bytes 3076
  33.2 3.1 %collective-permute-start.9 = (bf16[4,1152,128]{2,1,0:T(8,128)(2,1)S(1)}, bf16[4,1152,128]{2,1,0:T(8,128)(2,1)S(1)}, u32[]{:S(2)}, u32[]{:S(2)}) collective-permute-start(bf16[4,1152,128]{2,1,0:T(8,128)(2,1)S(1)} %pad_maximum_fusion.refs_6_), channel_id=1, source_target_pairs={{0,4},{4,0},{8,12},{12,8},{16,20},{20,16},{24,28},{28,24},{1,5},{5... | collective-permute-start | bytes 3538952 | tf_op jit(solution)/shard_map/ppermute | solution.py:240

commit v4 on v3

--- a/solution.py
+++ b/solution.py
@@ -67,26 +67,21 @@
     return jnp.concatenate([values, jnp.ones((values.shape[0], LANES), BF16)], axis=1)
 
 
-def load_kernel(n, *refs):
-    sems = refs[2 * n]
-    moves = [pltpu.make_async_copy(refs[i], refs[n + i], sems.at[i]) for i in range(n)]
+def first_kernel(*refs):
+    given = refs[:5]
+    (w_in, pos, gain, own, b_in, cut, sems) = refs[5:]
+    moves = [pltpu.make_async_copy(a, b, sems.at[i]) for i, (a, b) in enumerate(zip(given, refs[5:10]))]
     for move in moves:
         move.start()
     for move in moves:
         move.wait()
-
-
-def own_kernel(slots, places, count, n_patch, *refs):
+    cut[...] = pos[:, pl.ds(pl.multiple_of(lax.axis_index("dp") * LANES, LANES), LANES)]
+
+
+def parts_kernel(slots, places, count, n_patch, *refs):
     patch_refs = refs[:n_patch]
-    (w_in, b_in, pos, gain) = refs[n_patch : n_patch + 4]
-    given = refs[n_patch + 4 : n_patch + 7]
-    (hidden_out, query_out, acc_out, top_out, parts_out, flipped_out, w_key, w_value) = refs[n_patch + 7 : n_patch + 15]
-    (held, w_query, sems) = refs[n_patch + 15 :]
-    moves = [pltpu.make_async_copy(a, b, sems.at[i]) for i, (a, b) in enumerate(zip(given, (w_query, w_key, w_value)))]
-    for move in moves:
-        move.start()
-    rows = pos.shape[0]
-    head = w_query.shape[1] // H
+    (w_in, b_in, parts_out, held) = refs[n_patch:]
+    rows = parts_out.shape[1]
     me = lax.axis_index("seq")
     place_patches(slots, patch_refs, held, rows, me)
     if slots is None:
@@ -100,17 +95,24 @@
         for i, place in enumerate(places):
             block = jnp.bitwise_xor(me, place)
             parts_out[i] = from_patches(window(held, block, rows, count), w_in[...], b_in[...])
+
+
+def own_kernel(slots, count, n_patch, *refs):
+    patch_refs = refs[:n_patch]
+    (w_in, b_in, pos, gain, w_query, w_key, w_value) = refs[n_patch : n_patch + 7]
+    (hidden_out, query_out, acc_out, top_out, flipped_out, held) = refs[n_patch + 7 :]
+    rows = pos.shape[0]
+    head = w_query.shape[1] // H
+    me = lax.axis_index("seq")
+    place_patches(slots, patch_refs, held, rows, me)
     own = window(held, me, rows, count)
     flipped_out[...] = reverse(own, rows - 1)
     hidden = from_patches(own, w_in[...], b_in[...]) + pos[...].astype(F32)
     hidden_out[...] = hidden
     normed = normalize(hidden, gain[...]).astype(BF16)
     scale = math.log2(math.e) / math.sqrt(head)
-    moves[0].wait()
     query_out[...] = (dot(normed, w_query[...]) * scale).astype(BF16)
-    moves[1].wait()
     keys = dot(normed, w_key[...]).astype(BF16)
-    moves[2].wait()
     values = dot(normed, w_value[...]).astype(BF16)
     row = lax.broadcasted_iota(jnp.int32, (rows, rows), 0)
     col = lax.broadcasted_iota(jnp.int32, (rows, rows), 1)
@@ -233,8 +235,17 @@
     b_in, ln_gain, out_gain, b_out = [a.reshape(1, -1) for a in (b_in, ln_gain, out_gain, b_out)]
     quick = count == 4 and groups == 8 and width == groups * LANES
     if quick:
-        group = lax.axis_index("dp")
-        cut = lax.dynamic_slice_in_dim(pos_embed, group * LANES, LANES, 1)
+        given = (w_in, pos_embed, ln_gain, patches, b_in)
+        w_in, pos_embed, ln_gain, patches, b_in, cut = pl.pallas_call(
+            first_kernel,
+            out_shape=[VMEM(a.shape, a.dtype) for a in (*given, patches)],
+            in_specs=spec(5, HBM),
+            out_specs=spec(6),
+            scratch_shapes=[pltpu.SemaphoreType.DMA((5,))],
+            compiler_params=pltpu.CompilerParams(vmem_limit_bytes=1 << 20),
+            cost_estimate=cost(1 << 34),
+            name="first_loads",
+        )(*[stay(a) for a in given])
 
         def swap(block, axis, mask, size):
             return lax.ppermute(block, axis, [(i, i ^ mask) for i in range(size)])
@@ -242,69 +253,57 @@
         def send(block, pairs):
             return lax.ppermute(block, "seq", pairs)
 
+        places = (3, 1, 2)
         along = [
             send(cut, [(2, 3), (0, 1)]),
             send(cut, [(1, 3), (0, 2)]),
             send(cut, [(0, 3), (1, 2)]),
         ]
-        after = lax.optimization_barrier((patches, cut))[0]
+        mine = jnp.concatenate([along[m - 1] for m in places], axis=0)
+        plane = [mine] + [swap(mine, "dp", m, groups) for m in (2, 4, 6)]
+        later = lax.optimization_barrier((patches, mine))[0]
         patch_list = [
             patches,
-            send(after, [(2, 3), (3, 2)]),
-            send(after, [(1, 3), (3, 1)]),
-            send(after, [(0, 3), (1, 2), (2, 1), (3, 0)]),
+            send(later, [(2, 3), (3, 2)]),
+            send(patches, [(1, 3), (3, 1)]),
+            send(patches, [(0, 3), (1, 2), (2, 1), (3, 0)]),
         ]
         slots = (0, 1, 2, 3)
-        places = (1, 2, 3)
+        own_slots = (0, 2, 3)
+        own_patches = [patch_list[i] for i in own_slots]
     else:
-        slots = places = None
-        patch_list = [lax.all_gather(patches, "seq", axis=0, tiled=True)]
+        slots = places = own_slots = None
+        patch_list = own_patches = [lax.all_gather(patches, "seq", axis=0, tiled=True)]
         pos_list = [lax.all_gather(pos_embed, "seq", axis=0, tiled=False)]
-    own_given = (w_in, b_in, pos_embed, ln_gain)
-    if quick:
-        own_given = pl.pallas_call(
-            functools.partial(load_kernel, len(own_given)),
-            out_shape=[VMEM(a.shape, a.dtype) for a in own_given],
-            in_specs=spec(len(own_given), HBM),
-            out_specs=spec(len(own_given)),
-            scratch_shapes=[pltpu.SemaphoreType.DMA((len(own_given),))],
-            compiler_params=pltpu.CompilerParams(vmem_limit_bytes=1 << 20),
-            cost_estimate=cost(1),
-            name="load_weights",
-        )(*[stay(a) for a in own_given])
-        own_given = list(own_given)
-        *along, own_given[1] = lax.optimization_barrier((*along, own_given[1]))
-        *patch_list[1:], own_given[1] = lax.optimization_barrier((*patch_list[1:], own_given[1]))
-        mine = jnp.concatenate(along, axis=0)
-        plane = [mine] + [swap(mine, "dp", m, groups) for m in (2, 4, 6)]
-        ln_gain = own_given[3]
     here = VMEM if quick else jax.ShapeDtypeStruct
     state = (here((H, rows, head + LANES), F32), here((H, rows, LANES), F32))
-    n = len(patch_list)
-    hidden, query, acc, top, parts, flipped, w_key, w_value = pl.pallas_call(
-        functools.partial(own_kernel, slots, places, count, n),
-        out_shape=(
-            here((rows, width), F32),
-            here((rows, width), BF16),
-            *state,
-            here((count - 1, rows, width), F32),
-            here((rows, feats), F32),
-            here(w_key.shape, BF16),
-            here(w_value.shape, BF16),
-        ),
-        in_specs=spec(n + 4) + spec(3, HBM),
-        out_specs=spec(8),
-        scratch_shapes=[
-            VMEM((count * rows + PAD, feats), BF16),
-            VMEM(w_query.shape, BF16),
-            pltpu.SemaphoreType.DMA((3,)),
-        ],
-        compiler_params=pltpu.CompilerParams(vmem_limit_bytes=(20 if quick else 54) << 20),
+    held = VMEM((count * rows + PAD, feats), BF16)
+    n = len(own_patches)
+    hidden, query, acc, top, flipped = pl.pallas_call(
+        functools.partial(own_kernel, own_slots, count, n),
+        out_shape=(here((rows, width), F32), here((rows, width), BF16), *state, here((rows, feats), F32)),
+        in_specs=spec(n + 7),
+        out_specs=spec(5),
+        scratch_shapes=[held],
+        compiler_params=pltpu.CompilerParams(vmem_limit_bytes=(16 if quick else 48) << 20),
         cost_estimate=cost(1 << 36),
         name="own_block",
-    )(*patch_list, *own_given, *[stay(a) for a in (w_query, w_key, w_value)])
+    )(*own_patches, w_in, b_in, pos_embed, ln_gain, w_query, w_key, w_value)
+    n = len(patch_list)
     if quick:
-        query, *plane = lax.optimization_barrier((query, *plane))
+        patch_list[1], query = lax.optimization_barrier((patch_list[1], query))
+    parts = pl.pallas_call(
+        functools.partial(parts_kernel, slots, places, count, n),
+        out_shape=here((count - 1, rows, width), F32),
+        in_specs=spec(n + 2),
+        out_specs=spec(1)[0],
+        scratch_shapes=[held],
+        compiler_params=pltpu.CompilerParams(vmem_limit_bytes=(10 if quick else 48) << 20),
+        cost_estimate=cost(1 << 30),
+        name="patch_parts",
+    )(*patch_list, w_in, b_in)
+    if quick:
+        parts, *plane = lax.optimization_barrier((parts, *plane))
         plane = jnp.stack(plane)
         pos_list = (plane, swap(plane, "dp", 1, groups))
     n = len(pos_list)

time: 50.6 us -> 49.3 us (0.974)
  the two profiles are of different devices: /device:TPU:19 before, /device:TPU:27 now
where the time goes in v4:
time: 49.3 us; the launch traced here: 49.1 us
  Pallas kernels  22.1 us (45%)
  starting transfers between devices  17.1 us (35%)
  waiting for transfers between devices  8.93 us (18%)
  between operations  0.85 us (2%)
    pallas_call x1, Pallas kernels, shards(): pl.pallas_call(functools.partial(rest_kernel, places, n), out_shape=(jax....  13.8 us
    ppermute x6, starting transfers between devices, send(): return lax.ppermute(block, 'seq', pairs)  13.7 us
    ppermute x4, waiting for transfers between devices, swap(): return lax.ppermute(block, axis, [(i, i ^ mask) for i in range(size)])  6.07 us
    pallas_call x1, Pallas kernels, shards(): pl.pallas_call(functools.partial(own_kernel, own_slots, count, n), out_sh...  5.23 us
    ppermute x4, starting transfers between devices, swap(): return lax.ppermute(block, axis, [(i, i ^ mask) for i in range(size)])  3.37 us
    ppermute x6, waiting for transfers between devices, send(): return lax.ppermute(block, 'seq', pairs)  2.86 us
    pallas_call x1, Pallas kernels, shards(): pl.pallas_call(functools.partial(parts_kernel, slots, places, count, n),...  1.62 us
    pallas_call x1, Pallas kernels, shards(): pl.pallas_call(first_kernel, out_shape=[VMEM(a.shape, a.dtype) for a in (...  1.45 us
  transfers between devices with their start and end apart: 10, of which 3 were waited for; matrix products, arithmetic and copies ran while one was open for 0% of the time, Pallas kernels for 14%

profile of v4, /device:TPU:27, one launch (start us, length us, event | category | flops | bytes accessed | tf_op | source)
XLA Modules:
  0.0 49.1 jit_solution(13606160273916165926)
XLA Ops:
  0.6 0.0 copy-start
  0.6 0.0 copy-start.1
  0.7 0.0 copy-start.6
  0.7 1.4 %first_loads.1 = (bf16[128,1024]{1,0:T(8,128)(2,1)S(1)}, bf16[384,1024]{1,0:T(8,128)(2,1)S(1)}, f32[1,1024]{1,0:T(1,128)S(1)}, bf16[384,128]{1,0:T(8,128)(2,1)S(...) custom-call(bf16[128,1024]{1,0:T(8,128)(2,1)} %refs_0_.1, bf16[384,1024]{1,0:T(8,128)(2,1)} %refs_1_.1, ...), custom_call_target="tpu_custom_call" | custom-call | flops 17179869184 | bytes 1048576 | tf_op jit(solution)/shard_map/first_loads/pallas_call | solution.py:239
  2.1 1.4 %collective-permute-start.2 = (bf16[384,128]{1,0:T(8,128)(2,1)S(1)}, bf16[384,128]{1,0:T(8,128)(2,1)S(1)}, u32[]{:S(2)}, u32[]{:S(2)}) collective-permute-start(bf16[384,128]{1,0:T(8,128)(2,1)S(1)} %get-tuple-element.29), channel_id=1, source_target_pairs={{0,3},{1,2},{4,7},{5,6},{8,11},{9,10},{12,15},{13,14},{16,19},{17,... | collective-permute-start | bytes 294920 | tf_op jit(solution)/shard_map/ppermute | solution.py:254
  3.5 1.3 %collective-permute-start.4 = (bf16[384,128]{1,0:T(8,128)(2,1)S(1)}, bf16[384,128]{1,0:T(8,128)(2,1)S(1)}, u32[]{:S(2)}, u32[]{:S(2)}) collective-permute-start(bf16[384,128]{1,0:T(8,128)(2,1)S(1)} %get-tuple-element.29), channel_id=1, source_target_pairs={{1,3},{0,2},{5,7},{4,6},{9,11},{8,10},{13,15},{12,14},{17,19},{16,... | collective-permute-start | bytes 294920 | tf_op jit(solution)/shard_map/ppermute | solution.py:254
  4.8 1.3 %collective-permute-start.3 = (bf16[384,128]{1,0:T(8,128)(2,1)S(1)}, bf16[384,128]{1,0:T(8,128)(2,1)S(1)}, u32[]{:S(2)}, u32[]{:S(2)}) collective-permute-start(bf16[384,128]{1,0:T(8,128)(2,1)S(1)} %get-tuple-element.29), channel_id=1, source_target_pairs={{2,3},{0,1},{6,7},{4,5},{10,11},{8,9},{14,15},{12,13},{18,19},{16,... | collective-permute-start | bytes 294920 | tf_op jit(solution)/shard_map/ppermute | solution.py:254
  6.1 4.8 %collective-permute-start.1 = (bf16[384,128]{1,0:T(8,128)(2,1)S(1)}, bf16[384,128]{1,0:T(8,128)(2,1)S(1)}, u32[]{:S(2)}, u32[]{:S(2)}) collective-permute-start(bf16[384,128]{1,0:T(8,128)(2,1)S(1)} %get-tuple-element.30.refs_0_), channel_id=1, source_target_pairs={{0,3},{1,2},{2,1},{3,0},{4,7},{5,6},{6,5},{7,4},{8,11},{9,10},{10,... | collective-permute-start | bytes 294920 | tf_op jit(solution)/shard_map/ppermute | solution.py:254
  11.0 1.9 %collective-permute-start = (bf16[384,128]{1,0:T(8,128)(2,1)S(1)}, bf16[384,128]{1,0:T(8,128)(2,1)S(1)}, u32[]{:S(2)}, u32[]{:S(2)}) collective-permute-start(bf16[384,128]{1,0:T(8,128)(2,1)S(1)} %get-tuple-element.30.refs_0_), channel_id=1, source_target_pairs={{1,3},{3,1},{5,7},{7,5},{9,11},{11,9},{13,15},{15,13},{17,19},{19,... | collective-permute-start | bytes 294920 | tf_op jit(solution)/shard_map/ppermute | solution.py:254
  12.9 0.0 collective-permute-done.2
  12.9 0.0 collective-permute-done.3
  13.0 2.8 %collective-permute-done.4 = bf16[384,128]{1,0:T(8,128)(2,1)S(1)} collective-permute-done((bf16[384,128]{1,0:T(8,128)(2,1)S(1)}, bf16[384,128]{1,0:T(8,128)(2,1)S(1)}, u32[]{:S(2)}, u32[]{:S(2)}) %collective-permute-start.4) | collective-permute-done | bytes 98336 | tf_op jit(solution)/shard_map/ppermute | solution.py:254
  15.8 1.3 %collective-permute-start.8 = (bf16[1152,128]{1,0:T(8,128)(2,1)S(1)}, bf16[1152,128]{1,0:T(8,128)(2,1)S(1)}, u32[]{:S(2)}, u32[]{:S(2)}) collective-permute-start(bf16[1152,128]{1,0:T(8,128)(2,1)S(1)} %constant_dynamic-update-slice_fusion), channel_id=1, source_target_pairs={{0,24},{4,28},{8,16},{12,20},{16,8},{20,12},{24,0},{28,4},{1,25},{... | collective-permute-start | bytes 884744 | tf_op jit(solution)/shard_map/ppermute | solution.py:251
  17.1 0.2 collective-permute-start.7
  17.3 1.2 %collective-permute-start.6 = (bf16[1152,128]{1,0:T(8,128)(2,1)S(1)}, bf16[1152,128]{1,0:T(8,128)(2,1)S(1)}, u32[]{:S(2)}, u32[]{:S(2)}) collective-permute-start(bf16[1152,128]{1,0:T(8,128)(2,1)S(1)} %constant_dynamic-update-slice_fusion), channel_id=1, source_target_pairs={{0,8},{4,12},{8,0},{12,4},{16,24},{20,28},{24,16},{28,20},{1,9},{5... | collective-permute-start | bytes 884744 | tf_op jit(solution)/shard_map/ppermute | solution.py:251
  18.6 0.0 collective-permute-done.1.refs_2_.refs_3_
  18.6 2.9 %collective-permute-start.5 = (bf16[384,128]{1,0:T(8,128)(2,1)S(1)}, bf16[384,128]{1,0:T(8,128)(2,1)S(1)}, u32[]{:S(2)}, u32[]{:S(2)}) collective-permute-start(bf16[384,128]{1,0:T(8,128)(2,1)S(1)} %get-tuple-element.30.refs_0_), channel_id=1, source_target_pairs={{2,3},{3,2},{6,7},{7,6},{10,11},{11,10},{14,15},{15,14},{18,19},{1... | collective-permute-start | bytes 294920 | tf_op jit(solution)/shard_map/ppermute | solution.py:254
  21.5 0.0 collective-permute-done.refs_1_.refs_2_
  21.5 0.0 copy-done
  21.5 0.0 copy-done.1
  21.5 0.0 copy-done.6
  21.5 5.2 %own_block.1 = (f32[384,1024]{1,0:T(8,128)S(1)}, bf16[384,1024]{1,0:T(8,128)(2,1)S(1)}, f32[8,384,256]{2,1,0:T(8,128)S(1)}, f32[8,384,128]{2,1,0:T(8,128)S(1)}, f32[384,128]{1,0:T(8,128)S(1)}) custom-call(bf16[384,128]{1,0:T(8,128)(2,1)S(1)} %get-tuple-element.30.refs_0_, bf16[384,128]{1,0:T(8,128)(2,1)S(1)} %collective-permute-done.refs_1_.refs_2_, ...), custom_call_target="tpu_custom_call" | custom-call | flops 68719476736 | bytes 1048576 | tf_op jit(solution)/shard_map/own_block/pallas_call | solution.py:282
  26.8 0.0 collective-permute-done.5.refs_1_
  26.8 0.0 copy-start.3
  26.8 1.6 %patch_parts.1.refs_4_ = f32[3,384,1024]{2,1,0:T(8,128)S(1)} custom-call(bf16[384,128]{1,0:T(8,128)(2,1)S(1)} %get-tuple-element.30.refs_0_, bf16[384,128]{1,0:T(8,128)(2,1)S(1)} %collective-permute-done.5.refs_1_, bf16[384,128]{1,0:T(8,128)(2,1)S(1)} %collective-permute-done.refs_1_.refs_2_, bf16[384,128]{1,0:T(8,128)(2,1)S(1)} %collective-permute-done.1.refs_2_.refs_3_, ...), custom_call_target="tpu_custom_call" | custom-call | flops 1073741824 | bytes 1048576 | tf_op jit(solution)/shard_map/patch_parts/pallas_call | solution.py:295
  28.4 0.0 copy-start.2
  28.4 0.0 copy-start.4
  28.4 0.0 copy-start.5
  28.5 0.0 collective-permute-done.8
  28.5 3.6 %collective-permute-done.7 = bf16[1152,128]{1,0:T(8,128)(2,1)S(1)} collective-permute-done((bf16[1152,128]{1,0:T(8,128)(2,1)S(1)}, bf16[1152,128]{1,0:T(8,128)(2,1)S(1)}, u32[]{:S(2)}, u32[]{:S(2)}) %collective-permute-start.7) | collective-permute-done | bytes 294944 | tf_op jit(solution)/shard_map/ppermute | solution.py:251
  32.1 0.0 collective-permute-done.6
  32.1 0.1 pad_maximum_fusion.refs_6_
  32.2 0.7 %collective-permute-start.9 = (bf16[4,1152,128]{2,1,0:T(8,128)(2,1)S(1)}, bf16[4,1152,128]{2,1,0:T(8,128)(2,1)S(1)}, u32[]{:S(2)}, u32[]{:S(2)}) collective-permute-start(bf16[4,1152,128]{2,1,0:T(8,128)(2,1)S(1)} %pad_maximum_fusion.refs_6_), channel_id=1, source_target_pairs={{0,4},{4,0},{8,12},{12,8},{16,20},{20,16},{24,28},{28,24},{1,5},{5... | collective-permute-start | bytes 3538952 | tf_op jit(solution)/shard_map/ppermute | solution.py:251
  32.9 2.5 %collective-permute-done.9.refs_7_ = bf16[4,1152,128]{2,1,0:T(8,128)(2,1)S(1)} collective-permute-done((bf16[4,1152,128]{2,1,0:T(8,128)(2,1)S(1)}, bf16[4,1152,128]{2,1,0:T(8,128)(2,1)S(1)}, u32[]{:S(2)}, u32[]{:S(2)}) %collective-permute-start.9) | collective-permute-done | bytes 1179680 | tf_op jit(solution)/shard_map/ppermute | solution.py:251
  35.3 0.0 copy-done.3
  35.3 0.0 copy-done.2
  35.3 0.0 copy-done.4
  35.3 0.0 copy-done.5
  35.4 13.8 %other_blocks.1 = (f32[384,128]{1,0:T(8,128)}, f32[384]{0:T(512)}, f32[8,384,256]{2,1,0:T(8,128)S(1)}, f32[8,384,128]{2,1,0:T(8,128)S(1)}) custom-call(f32[384,1024]{1,0:T(8,128)S(1)} %get-tuple-element.28.refs_0_, bf16[384,1024]{1,0:T(8,128)(2,1)S(1)} %get-tuple-element.32.refs_1_, ...), custom_call_target="tpu_custom_call", output_to_operand_aliasing={{2}: (2, {}), {3}: (3, {})} | custom-call | flops 1 | bytes 1048576 | tf_op jit(solution)/shard_map/other_blocks/pallas_call | solution.py:310
  (3 shorter events, 0.0 us)
Async XLA Ops:
  0.6 20.9 %copy-start = (bf16[1024,1024]{1,0:T(8,128)(2,1)S(1)}, bf16[1024,1024]{1,0:T(8,128)(2,1)}, u32[]{:S(2)}) copy-start(bf16[1024,1024]{1,0:T(8,128)(2,1)} %refs_9_.3) | copy-start | bytes 6291460
  0.6 20.9 %copy-start.1 = (bf16[1024,1024]{1,0:T(8,128)(2,1)S(1)}, bf16[1024,1024]{1,0:T(8,128)(2,1)}, u32[]{:S(2)}) copy-start(bf16[1024,1024]{1,0:T(8,128)(2,1)} %refs_10_.1) | copy-start | bytes 6291460
  0.7 20.9 %copy-start.6 = (bf16[1024,1024]{1,0:T(8,128)(2,1)S(1)}, bf16[1024,1024]{1,0:T(8,128)(2,1)}, u32[]{:S(2)}) copy-start(bf16[1024,1024]{1,0:T(8,128)(2,1)} %refs_7_.1) | copy-start | bytes 6291460
  2.1 10.8 %collective-permute-start.2 = (bf16[384,128]{1,0:T(8,128)(2,1)S(1)}, bf16[384,128]{1,0:T(8,128)(2,1)S(1)}, u32[]{:S(2)}, u32[]{:S(2)}) collective-permute-start(bf16[384,128]{1,0:T(8,128)(2,1)S(1)} %get-tuple-element.29), channel_id=1, source_target_pairs={{0,3},{1,2},{4,7},{5,6},{8,11},{9,10},{12,15},{13,14},{16,19},{17,... | collective-permute-start | bytes 294920 | tf_op jit(solution)/shard_map/ppermute | solution.py:254
  3.5 12.3 %collective-permute-start.4 = (bf16[384,128]{1,0:T(8,128)(2,1)S(1)}, bf16[384,128]{1,0:T(8,128)(2,1)S(1)}, u32[]{:S(2)}, u32[]{:S(2)}) collective-permute-start(bf16[384,128]{1,0:T(8,128)(2,1)S(1)} %get-tuple-element.29), channel_id=1, source_target_pairs={{1,3},{0,2},{5,7},{4,6},{9,11},{8,10},{13,15},{12,14},{17,19},{16,... | collective-permute-start | bytes 294920 | tf_op jit(solution)/shard_map/ppermute | solution.py:254
  4.8 8.1 %collective-permute-start.3 = (bf16[384,128]{1,0:T(8,128)(2,1)S(1)}, bf16[384,128]{1,0:T(8,128)(2,1)S(1)}, u32[]{:S(2)}, u32[]{:S(2)}) collective-permute-start(bf16[384,128]{1,0:T(8,128)(2,1)S(1)} %get-tuple-element.29), channel_id=1, source_target_pairs={{2,3},{0,1},{6,7},{4,5},{10,11},{8,9},{14,15},{12,13},{18,19},{16,... | collective-permute-start | bytes 294920 | tf_op jit(solution)/shard_map/ppermute | solution.py:254
  6.1 12.4 %collective-permute-start.1 = (bf16[384,128]{1,0:T(8,128)(2,1)S(1)}, bf16[384,128]{1,0:T(8,128)(2,1)S(1)}, u32[]{:S(2)}, u32[]{:S(2)}) collective-permute-start(bf16[384,128]{1,0:T(8,128)(2,1)S(1)} %get-tuple-element.30.refs_0_), channel_id=1, source_target_pairs={{0,3},{1,2},{2,1},{3,0},{4,7},{5,6},{6,5},{7,4},{8,11},{9,10},{10,... | collective-permute-start | bytes 294920 | tf_op jit(solution)/shard_map/ppermute | solution.py:254
  11.0 10.5 %collective-permute-start = (bf16[384,128]{1,0:T(8,128)(2,1)S(1)}, bf16[384,128]{1,0:T(8,128)(2,1)S(1)}, u32[]{:S(2)}, u32[]{:S(2)}) collective-permute-start(bf16[384,128]{1,0:T(8,128)(2,1)S(1)} %get-tuple-element.30.refs_0_), channel_id=1, source_target_pairs={{1,3},{3,1},{5,7},{7,5},{9,11},{11,9},{13,15},{15,13},{17,19},{19,... | collective-permute-start | bytes 294920 | tf_op jit(solution)/shard_map/ppermute | solution.py:254
  15.8 12.6 %collective-permute-start.8 = (bf16[1152,128]{1,0:T(8,128)(2,1)S(1)}, bf16[1152,128]{1,0:T(8,128)(2,1)S(1)}, u32[]{:S(2)}, u32[]{:S(2)}) collective-permute-start(bf16[1152,128]{1,0:T(8,128)(2,1)S(1)} %constant_dynamic-update-slice_fusion), channel_id=1, source_target_pairs={{0,24},{4,28},{8,16},{12,20},{16,8},{20,12},{24,0},{28,4},{1,25},{... | collective-permute-start | bytes 884744 | tf_op jit(solution)/shard_map/ppermute | solution.py:251
  17.1 14.9 %collective-permute-start.7 = (bf16[1152,128]{1,0:T(8,128)(2,1)S(1)}, bf16[1152,128]{1,0:T(8,128)(2,1)S(1)}, u32[]{:S(2)}, u32[]{:S(2)}) collective-permute-start(bf16[1152,128]{1,0:T(8,128)(2,1)S(1)} %constant_dynamic-update-slice_fusion), channel_id=1, source_target_pairs={{0,16},{4,20},{8,24},{12,28},{16,0},{20,4},{24,8},{28,12},{1,17},{... | collective-permute-start | bytes 884744 | tf_op jit(solution)/shard_map/ppermute | solution.py:251
  17.3 14.7 %collective-permute-start.6 = (bf16[1152,128]{1,0:T(8,128)(2,1)S(1)}, bf16[1152,128]{1,0:T(8,128)(2,1)S(1)}, u32[]{:S(2)}, u32[]{:S(2)}) collective-permute-start(bf16[1152,128]{1,0:T(8,128)(2,1)S(1)} %constant_dynamic-update-slice_fusion), channel_id=1, source_target_pairs={{0,8},{4,12},{8,0},{12,4},{16,24},{20,28},{24,16},{28,20},{1,9},{5... | collective-permute-start | bytes 884744 | tf_op jit(solution)/shard_map/ppermute | solution.py:251
  18.6 8.2 %collective-permute-start.5 = (bf16[384,128]{1,0:T(8,128)(2,1)S(1)}, bf16[384,128]{1,0:T(8,128)(2,1)S(1)}, u32[]{:S(2)}, u32[]{:S(2)}) collective-permute-start(bf16[384,128]{1,0:T(8,128)(2,1)S(1)} %get-tuple-element.30.refs_0_), channel_id=1, source_target_pairs={{2,3},{3,2},{6,7},{7,6},{10,11},{11,10},{14,15},{15,14},{18,19},{1... | collective-permute-start | bytes 294920 | tf_op jit(solution)/shard_map/ppermute | solution.py:254
  26.8 8.6 %copy-start.3 = (bf16[1024,256]{1,0:T(8,128)(2,1)S(1)}, bf16[1024,256]{1,0:T(8,128)(2,1)}, u32[]{:S(2)}) copy-start(bf16[1024,256]{1,0:T(8,128)(2,1)} %refs_13_.1) | copy-start | bytes 1572868
  28.4 6.9 %copy-start.2 = (bf16[1024,1024]{1,0:T(8,128)(2,1)S(1)}, bf16[1024,1024]{1,0:T(8,128)(2,1)}, u32[]{:S(2)}) copy-start(bf16[1024,1024]{1,0:T(8,128)(2,1)} %refs_11_.1) | copy-start | bytes 6291460
  28.4 6.9 %copy-start.4 = (f32[1024]{0:T(1024)S(1)}, f32[1024]{0:T(1024)}, u32[]{:S(2)}) copy-start(f32[1024]{0:T(1024)} %param.21) | copy-start | bytes 12292
  28.4 6.9 %copy-start.5 = (f32[256]{0:T(256)S(1)}, f32[256]{0:T(256)}, u32[]{:S(2)}) copy-start(f32[256]{0:T(256)} %param.23) | copy-start | bytes 3076
  32.2 3.1 %collective-permute-start.9 = (bf16[4,1152,128]{2,1,0:T(8,128)(2,1)S(1)}, bf16[4,1152,128]{2,1,0:T(8,128)(2,1)S(1)}, u32[]{:S(2)}, u32[]{:S(2)}) collective-permute-start(bf16[4,1152,128]{2,1,0:T(8,128)(2,1)S(1)} %pad_maximum_fusion.refs_6_), channel_id=1, source_target_pairs={{0,4},{4,0},{8,12},{12,8},{16,20},{20,16},{24,28},{28,24},{1,5},{5... | collective-permute-start | bytes 3538952 | tf_op jit(solution)/shard_map/ppermute | solution.py:251

commit v5 on v4

--- a/solution.py
+++ b/solution.py
@@ -68,14 +68,14 @@
 
 
 def first_kernel(*refs):
-    given = refs[:5]
-    (w_in, pos, gain, own, b_in, cut, sems) = refs[5:]
-    moves = [pltpu.make_async_copy(a, b, sems.at[i]) for i, (a, b) in enumerate(zip(given, refs[5:10]))]
+    given, pos, targets, sems = refs[:4], refs[4], refs[5:10], refs[10]
+    columns = pl.ds(pl.multiple_of(lax.axis_index("dp") * LANES, LANES), LANES)
+    sources = (*given, pos.at[:, columns])
+    moves = [pltpu.make_async_copy(a, b, sems.at[i]) for i, (a, b) in enumerate(zip(sources, targets))]
     for move in moves:
         move.start()
     for move in moves:
         move.wait()
-    cut[...] = pos[:, pl.ds(pl.multiple_of(lax.axis_index("dp") * LANES, LANES), LANES)]
 
 
 def parts_kernel(slots, places, count, n_patch, *refs):
@@ -174,11 +174,13 @@
         acc[h] = acc[h] * repeat(factor, head + LANES) + dot(weights, with_ones(values[:, h * head : (h + 1) * head]))
 
 
-def place_positions(mine, other, pos_held):
+def place_positions(mine, near, plane, other, pos_held):
     group = lax.axis_index("dp")
-    for i in range(mine.shape[0]):
-        pos_held[jnp.bitwise_xor(group, 2 * i)] = mine[i]
-        pos_held[jnp.bitwise_xor(group, 2 * i + 1)] = other[i]
+    pos_held[group] = mine[...]
+    pos_held[jnp.bitwise_xor(group, 1)] = near[...]
+    for i in range(plane.shape[0]):
+        pos_held[jnp.bitwise_xor(group, 2 * i + 2)] = plane[i]
+        pos_held[jnp.bitwise_xor(group, 2 * i + 3)] = other[i]
 
 
 def rest_kernel(places, n_pos, *refs):
@@ -235,17 +237,17 @@
     b_in, ln_gain, out_gain, b_out = [a.reshape(1, -1) for a in (b_in, ln_gain, out_gain, b_out)]
     quick = count == 4 and groups == 8 and width == groups * LANES
     if quick:
-        given = (w_in, pos_embed, ln_gain, patches, b_in)
-        w_in, pos_embed, ln_gain, patches, b_in, cut = pl.pallas_call(
+        given = (w_in, ln_gain, patches, b_in)
+        w_in, ln_gain, patches, b_in, cut = pl.pallas_call(
             first_kernel,
             out_shape=[VMEM(a.shape, a.dtype) for a in (*given, patches)],
             in_specs=spec(5, HBM),
-            out_specs=spec(6),
+            out_specs=spec(5),
             scratch_shapes=[pltpu.SemaphoreType.DMA((5,))],
             compiler_params=pltpu.CompilerParams(vmem_limit_bytes=1 << 20),
             cost_estimate=cost(1 << 34),
             name="first_loads",
-        )(*[stay(a) for a in given])
+        )(*[stay(a) for a in (*given, pos_embed)])
 
         def swap(block, axis, mask, size):
             return lax.ppermute(block, axis, [(i, i ^ mask) for i in range(size)])
@@ -292,6 +294,8 @@
     n = len(patch_list)
     if quick:
         patch_list[1], query = lax.optimization_barrier((patch_list[1], query))
+        near = swap(mine, "dp", 1, groups)
+        near, b_in = lax.optimization_barrier((near, b_in))
     parts = pl.pallas_call(
         functools.partial(parts_kernel, slots, places, count, n),
         out_shape=here((count - 1, rows, width), F32),
@@ -304,8 +308,8 @@
     )(*patch_list, w_in, b_in)
     if quick:
         parts, *plane = lax.optimization_barrier((parts, *plane))
-        plane = jnp.stack(plane)
-        pos_list = (plane, swap(plane, "dp", 1, groups))
+        plane = jnp.stack(plane[1:])
+        pos_list = (mine, near, plane, swap(plane, "dp", 1, groups))
     n = len(pos_list)
     latent, logdet, _, _ = pl.pallas_call(
         functools.partial(rest_kernel, places, n),

time: 49.3 us -> 48.8 us (0.990)
  waiting for transfers between devices: 8.93 us -> 6.59 us
  starting transfers between devices: 17.1 us -> 19.1 us
    ppermute x4 -> x5, starting transfers between devices: 3.37 us -> 6.29 us  [swap(): return lax.ppermute(block, axis, [(i, i ^ mask) for i in range(size)])]
    ppermute x4 -> x5, waiting for transfers between devices: 6.07 us -> 3.73 us  [swap(): return lax.ppermute(block, axis, [(i, i ^ mask) for i in range(size)])]
    ppermute x6, starting transfers between devices: 13.7 us -> 12.8 us  [send(): return lax.ppermute(block, 'seq', pairs)]
  transfers between devices with their start and end apart: 10 -> 11, of which waited for: 3 -> 3; matrix products, arithmetic and copies ran while one was open for 0% -> 0% of each run, Pallas kernels for 14% -> 14%
where the time goes in v5:
time: 48.8 us; the launch traced here: 48.6 us
  Pallas kernels  21.9 us (45%)
  starting transfers between devices  19.1 us (39%)
  waiting for transfers between devices  6.59 us (14%)
  between operations  0.86 us (2%)
    pallas_call x1, Pallas kernels, shards(): pl.pallas_call(functools.partial(rest_kernel, places, n), out_shape=(jax....  13.8 us
    ppermute x6, starting transfers between devices, send(): return lax.ppermute(block, 'seq', pairs)  12.8 us
    ppermute x5, starting transfers between devices, swap(): return lax.ppermute(block, axis, [(i, i ^ mask) for i in range(size)])  6.29 us
    pallas_call x1, Pallas kernels, shards(): pl.pallas_call(functools.partial(own_kernel, own_slots, count, n), out_sh...  5.23 us
    ppermute x5, waiting for transfers between devices, swap(): return lax.ppermute(block, axis, [(i, i ^ mask) for i in range(size)])  3.73 us
    ppermute x6, waiting for transfers between devices, send(): return lax.ppermute(block, 'seq', pairs)  2.86 us
    pallas_call x1, Pallas kernels, shards(): pl.pallas_call(functools.partial(parts_kernel, slots, places, count, n),...  1.62 us
    pallas_call x1, Pallas kernels, shards(): pl.pallas_call(first_kernel, out_shape=[VMEM(a.shape, a.dtype) for a in (...  1.25 us
  transfers between devices with their start and end apart: 11, of which 3 were waited for; matrix products, arithmetic and copies ran while one was open for 0% of the time, Pallas kernels for 14%

profile of v5, /device:TPU:27, one launch (start us, length us, event | category | flops | bytes accessed | tf_op | source)
XLA Modules:
  0.0 48.6 jit_solution(17427806409731756909)
XLA Ops:
  0.6 0.0 copy-start
  0.6 0.0 copy-start.1
  0.7 0.0 copy-start.6
  0.7 0.0 copy-start.7
  0.7 1.2 %first_loads.1 = (bf16[128,1024]{1,0:T(8,128)(2,1)S(1)}, f32[1,1024]{1,0:T(1,128)S(1)}, bf16[384,128]{1,0:T(8,128)(2,1)S(1)}, f32[1,1024]{1,0:T(1,128)S(1)}, bf16[384,128]{1,0:T(8,128)(2,1)S(1)}) custom-call(bf16[128,1024]{1,0:T(8,128)(2,1)} %refs_0_.1, f32[1,1024]{1,0:T(1,128)} %bitcast.12, bf16[384,128]{1,0:T(8,128)(2,1)} %refs_2_.1, f32[1,1024]{1,0:T(1,128)} %bitcast.13, ...), custom_call_target="tpu_custom_call" | custom-call | flops 17179869184 | bytes 1048576 | tf_op jit(solution)/shard_map/first_loads/pallas_call | solution.py:241
  1.9 1.6 %collective-permute-start.2 = (bf16[384,128]{1,0:T(8,128)(2,1)S(1)}, bf16[384,128]{1,0:T(8,128)(2,1)S(1)}, u32[]{:S(2)}, u32[]{:S(2)}) collective-permute-start(bf16[384,128]{1,0:T(8,128)(2,1)S(1)} %get-tuple-element.28), channel_id=1, source_target_pairs={{0,3},{1,2},{4,7},{5,6},{8,11},{9,10},{12,15},{13,14},{16,19},{17,... | collective-permute-start | bytes 294920 | tf_op jit(solution)/shard_map/ppermute | solution.py:256
  3.5 1.3 %collective-permute-start.4 = (bf16[384,128]{1,0:T(8,128)(2,1)S(1)}, bf16[384,128]{1,0:T(8,128)(2,1)S(1)}, u32[]{:S(2)}, u32[]{:S(2)}) collective-permute-start(bf16[384,128]{1,0:T(8,128)(2,1)S(1)} %get-tuple-element.28), channel_id=1, source_target_pairs={{1,3},{0,2},{5,7},{4,6},{9,11},{8,10},{13,15},{12,14},{17,19},{16,... | collective-permute-start | bytes 294920 | tf_op jit(solution)/shard_map/ppermute | solution.py:256
  4.8 1.3 %collective-permute-start.3 = (bf16[384,128]{1,0:T(8,128)(2,1)S(1)}, bf16[384,128]{1,0:T(8,128)(2,1)S(1)}, u32[]{:S(2)}, u32[]{:S(2)}) collective-permute-start(bf16[384,128]{1,0:T(8,128)(2,1)S(1)} %get-tuple-element.28), channel_id=1, source_target_pairs={{2,3},{0,1},{6,7},{4,5},{10,11},{8,9},{14,15},{12,13},{18,19},{16,... | collective-permute-start | bytes 294920 | tf_op jit(solution)/shard_map/ppermute | solution.py:256
  6.1 4.8 %collective-permute-start.1 = (bf16[384,128]{1,0:T(8,128)(2,1)S(1)}, bf16[384,128]{1,0:T(8,128)(2,1)S(1)}, u32[]{:S(2)}, u32[]{:S(2)}) collective-permute-start(bf16[384,128]{1,0:T(8,128)(2,1)S(1)} %get-tuple-element.29.refs_0_), channel_id=1, source_target_pairs={{0,3},{1,2},{2,1},{3,0},{4,7},{5,6},{6,5},{7,4},{8,11},{9,10},{10,... | collective-permute-start | bytes 294920 | tf_op jit(solution)/shard_map/ppermute | solution.py:256
  10.9 1.9 %collective-permute-start = (bf16[384,128]{1,0:T(8,128)(2,1)S(1)}, bf16[384,128]{1,0:T(8,128)(2,1)S(1)}, u32[]{:S(2)}, u32[]{:S(2)}) collective-permute-start(bf16[384,128]{1,0:T(8,128)(2,1)S(1)} %get-tuple-element.29.refs_0_), channel_id=1, source_target_pairs={{1,3},{3,1},{5,7},{7,5},{9,11},{11,9},{13,15},{15,13},{17,19},{19,... | collective-permute-start | bytes 294920 | tf_op jit(solution)/shard_map/ppermute | solution.py:256
  12.9 0.0 collective-permute-done.2
  12.9 0.0 collective-permute-done.3
  12.9 2.8 %collective-permute-done.4 = bf16[384,128]{1,0:T(8,128)(2,1)S(1)} collective-permute-done((bf16[384,128]{1,0:T(8,128)(2,1)S(1)}, bf16[384,128]{1,0:T(8,128)(2,1)S(1)}, u32[]{:S(2)}, u32[]{:S(2)}) %collective-permute-start.4) | collective-permute-done | bytes 98336 | tf_op jit(solution)/shard_map/ppermute | solution.py:256
  15.8 1.3 %collective-permute-start.9 = (bf16[1152,128]{1,0:T(8,128)(2,1)S(1)}, bf16[1152,128]{1,0:T(8,128)(2,1)S(1)}, u32[]{:S(2)}, u32[]{:S(2)}) collective-permute-start(bf16[1152,128]{1,0:T(8,128)(2,1)S(1)} %constant_dynamic-update-slice_fusion.refs_6_), channel_id=1, source_target_pairs={{0,24},{4,28},{8,16},{12,20},{16,8},{20,12},{24,0},{28,4},{1,25},{... | collective-permute-start | bytes 884744 | tf_op jit(solution)/shard_map/ppermute | solution.py:253
  17.1 0.2 collective-permute-start.8
  17.3 1.2 %collective-permute-start.7 = (bf16[1152,128]{1,0:T(8,128)(2,1)S(1)}, bf16[1152,128]{1,0:T(8,128)(2,1)S(1)}, u32[]{:S(2)}, u32[]{:S(2)}) collective-permute-start(bf16[1152,128]{1,0:T(8,128)(2,1)S(1)} %constant_dynamic-update-slice_fusion.refs_6_), channel_id=1, source_target_pairs={{0,8},{4,12},{8,0},{12,4},{16,24},{20,28},{24,16},{28,20},{1,9},{5... | collective-permute-start | bytes 884744 | tf_op jit(solution)/shard_map/ppermute | solution.py:253
  18.5 0.0 collective-permute-done.1.refs_2_.refs_3_
  18.5 2.9 %collective-permute-start.6 = (bf16[1152,128]{1,0:T(8,128)(2,1)S(1)}, bf16[1152,128]{1,0:T(8,128)(2,1)S(1)}, u32[]{:S(2)}, u32[]{:S(2)}) collective-permute-start(bf16[1152,128]{1,0:T(8,128)(2,1)S(1)} %constant_dynamic-update-slice_fusion.refs_6_), channel_id=1, source_target_pairs={{0,4},{4,0},{8,12},{12,8},{16,20},{20,16},{24,28},{28,24},{1,5},{5... | collective-permute-start | bytes 884744 | tf_op jit(solution)/shard_map/ppermute | solution.py:253
  21.4 0.0 collective-permute-done.refs_1_.refs_2_
  21.4 1.9 %collective-permute-start.5 = (bf16[384,128]{1,0:T(8,128)(2,1)S(1)}, bf16[384,128]{1,0:T(8,128)(2,1)S(1)}, u32[]{:S(2)}, u32[]{:S(2)}) collective-permute-start(bf16[384,128]{1,0:T(8,128)(2,1)S(1)} %get-tuple-element.29.refs_0_), channel_id=1, source_target_pairs={{2,3},{3,2},{6,7},{7,6},{10,11},{11,10},{14,15},{15,14},{18,19},{1... | collective-permute-start | bytes 294920 | tf_op jit(solution)/shard_map/ppermute | solution.py:256
  23.3 0.0 copy-done
  23.3 0.0 copy-done.1
  23.4 0.0 copy-done.6
  23.4 0.0 copy-done.7
  23.4 5.2 %own_block.1 = (f32[384,1024]{1,0:T(8,128)S(1)}, bf16[384,1024]{1,0:T(8,128)(2,1)S(1)}, f32[8,384,256]{2,1,0:T(8,128)S(1)}, f32[8,384,128]{2,1,0:T(8,128)S(1)}, f32[384,128]{1,0:T(8,128)S(1)}) custom-call(bf16[384,128]{1,0:T(8,128)(2,1)S(1)} %get-tuple-element.29.refs_0_, bf16[384,128]{1,0:T(8,128)(2,1)S(1)} %collective-permute-done.refs_1_.refs_2_, ...), custom_call_target="tpu_custom_call" | custom-call | flops 68719476736 | bytes 1048576 | tf_op jit(solution)/shard_map/own_block/pallas_call | solution.py:284
  28.6 0.0 collective-permute-done.5.refs_1_
  28.6 0.0 copy-start.4
  28.6 0.0 copy-start.5
  28.7 0.0 collective-permute-done.6.refs_7_
  28.7 0.0 copy-start.2
  28.7 1.6 %patch_parts.1.refs_4_ = f32[3,384,1024]{2,1,0:T(8,128)S(1)} custom-call(bf16[384,128]{1,0:T(8,128)(2,1)S(1)} %get-tuple-element.29.refs_0_, bf16[384,128]{1,0:T(8,128)(2,1)S(1)} %collective-permute-done.5.refs_1_, bf16[384,128]{1,0:T(8,128)(2,1)S(1)} %collective-permute-done.refs_1_.refs_2_, bf16[384,128]{1,0:T(8,128)(2,1)S(1)} %collective-permute-done.1.refs_2_.refs_3_, ...), custom_call_target="tpu_custom_call" | custom-call | flops 1073741824 | bytes 1048576 | tf_op jit(solution)/shard_map/patch_parts/pallas_call | solution.py:299
  30.3 0.0 copy-start.3
  30.3 0.0 collective-permute-done.9
  30.3 1.7 %collective-permute-done.8 = bf16[1152,128]{1,0:T(8,128)(2,1)S(1)} collective-permute-done((bf16[1152,128]{1,0:T(8,128)(2,1)S(1)}, bf16[1152,128]{1,0:T(8,128)(2,1)S(1)}, u32[]{:S(2)}, u32[]{:S(2)}) %collective-permute-start.8) | collective-permute-done | bytes 294944 | tf_op jit(solution)/shard_map/ppermute | solution.py:253
  32.0 0.0 collective-permute-done.7
  32.0 0.1 pad_maximum_fusion.refs_8_
  32.1 0.7 %collective-permute-start.10 = (bf16[3,1152,128]{2,1,0:T(8,128)(2,1)S(1)}, bf16[3,1152,128]{2,1,0:T(8,128)(2,1)S(1)}, u32[]{:S(2)}, u32[]{:S(2)}) collective-permute-start(bf16[3,1152,128]{2,1,0:T(8,128)(2,1)S(1)} %pad_maximum_fusion.refs_8_), channel_id=1, source_target_pairs={{0,4},{4,0},{8,12},{12,8},{16,20},{20,16},{24,28},{28,24},{1,5},{5... | collective-permute-start | bytes 2654216 | tf_op jit(solution)/shard_map/ppermute | solution.py:253
  32.8 2.1 %collective-permute-done.10.refs_9_ = bf16[3,1152,128]{2,1,0:T(8,128)(2,1)S(1)} collective-permute-done((bf16[3,1152,128]{2,1,0:T(8,128)(2,1)S(1)}, bf16[3,1152,128]{2,1,0:T(8,128)(2,1)S(1)}, u32[]{:S(2)}, u32[]{:S(2)}) %collective-permute-start.10) | collective-permute-done | bytes 884768 | tf_op jit(solution)/shard_map/ppermute | solution.py:253
  34.8 0.0 copy-done.4
  34.8 0.0 copy-done.5
  34.8 0.0 copy-done.2
  34.8 0.0 copy-done.3
  34.8 13.8 %other_blocks.1 = (f32[384,128]{1,0:T(8,128)}, f32[384]{0:T(512)}, f32[8,384,256]{2,1,0:T(8,128)S(1)}, f32[8,384,128]{2,1,0:T(8,128)S(1)}) custom-call(f32[384,1024]{1,0:T(8,128)S(1)} %get-tuple-element.27.refs_0_, bf16[384,1024]{1,0:T(8,128)(2,1)S(1)} %get-tuple-element.31.refs_1_, ...), custom_call_target="tpu_custom_call", output_to_operand_aliasing={{2}: (2, {}), {3}: (3, {})} | custom-call | flops 1 | bytes 1048576 | tf_op jit(solution)/shard_map/other_blocks/pallas_call | solution.py:314
  (3 shorter events, 0.0 us)
Async XLA Ops:
  0.6 22.7 %copy-start = (bf16[1024,1024]{1,0:T(8,128)(2,1)S(1)}, bf16[1024,1024]{1,0:T(8,128)(2,1)}, u32[]{:S(2)}) copy-start(bf16[1024,1024]{1,0:T(8,128)(2,1)} %refs_11_.1) | copy-start | bytes 6291460
  0.6 22.7 %copy-start.1 = (bf16[1024,1024]{1,0:T(8,128)(2,1)S(1)}, bf16[1024,1024]{1,0:T(8,128)(2,1)}, u32[]{:S(2)}) copy-start(bf16[1024,1024]{1,0:T(8,128)(2,1)} %refs_12_.1) | copy-start | bytes 6291460
  0.7 22.7 %copy-start.6 = (bf16[1024,1024]{1,0:T(8,128)(2,1)S(1)}, bf16[1024,1024]{1,0:T(8,128)(2,1)}, u32[]{:S(2)}) copy-start(bf16[1024,1024]{1,0:T(8,128)(2,1)} %refs_7_.1) | copy-start | bytes 6291460
  0.7 22.7 %copy-start.7 = (bf16[384,1024]{1,0:T(8,128)(2,1)S(1)}, bf16[384,1024]{1,0:T(8,128)(2,1)}, u32[]{:S(2)}) copy-start(bf16[384,1024]{1,0:T(8,128)(2,1)} %refs_5_.1) | copy-start | bytes 2359300
  1.9 10.9 %collective-permute-start.2 = (bf16[384,128]{1,0:T(8,128)(2,1)S(1)}, bf16[384,128]{1,0:T(8,128)(2,1)S(1)}, u32[]{:S(2)}, u32[]{:S(2)}) collective-permute-start(bf16[384,128]{1,0:T(8,128)(2,1)S(1)} %get-tuple-element.28), channel_id=1, source_target_pairs={{0,3},{1,2},{4,7},{5,6},{8,11},{9,10},{12,15},{13,14},{16,19},{17,... | collective-permute-start | bytes 294920 | tf_op jit(solution)/shard_map/ppermute | solution.py:256
  3.5 12.3 %collective-permute-start.4 = (bf16[384,128]{1,0:T(8,128)(2,1)S(1)}, bf16[384,128]{1,0:T(8,128)(2,1)S(1)}, u32[]{:S(2)}, u32[]{:S(2)}) collective-permute-start(bf16[384,128]{1,0:T(8,128)(2,1)S(1)} %get-tuple-element.28), channel_id=1, source_target_pairs={{1,3},{0,2},{5,7},{4,6},{9,11},{8,10},{13,15},{12,14},{17,19},{16,... | collective-permute-start | bytes 294920 | tf_op jit(solution)/shard_map/ppermute | solution.py:256
  4.8 8.1 %collective-permute-start.3 = (bf16[384,128]{1,0:T(8,128)(2,1)S(1)}, bf16[384,128]{1,0:T(8,128)(2,1)S(1)}, u32[]{:S(2)}, u32[]{:S(2)}) collective-permute-start(bf16[384,128]{1,0:T(8,128)(2,1)S(1)} %get-tuple-element.28), channel_id=1, source_target_pairs={{2,3},{0,1},{6,7},{4,5},{10,11},{8,9},{14,15},{12,13},{18,19},{16,... | collective-permute-start | bytes 294920 | tf_op jit(solution)/shard_map/ppermute | solution.py:256
  6.1 12.4 %collective-permute-start.1 = (bf16[384,128]{1,0:T(8,128)(2,1)S(1)}, bf16[384,128]{1,0:T(8,128)(2,1)S(1)}, u32[]{:S(2)}, u32[]{:S(2)}) collective-permute-start(bf16[384,128]{1,0:T(8,128)(2,1)S(1)} %get-tuple-element.29.refs_0_), channel_id=1, source_target_pairs={{0,3},{1,2},{2,1},{3,0},{4,7},{5,6},{6,5},{7,4},{8,11},{9,10},{10,... | collective-permute-start | bytes 294920 | tf_op jit(solution)/shard_map/ppermute | solution.py:256
  10.9 10.5 %collective-permute-start = (bf16[384,128]{1,0:T(8,128)(2,1)S(1)}, bf16[384,128]{1,0:T(8,128)(2,1)S(1)}, u32[]{:S(2)}, u32[]{:S(2)}) collective-permute-start(bf16[384,128]{1,0:T(8,128)(2,1)S(1)} %get-tuple-element.29.refs_0_), channel_id=1, source_target_pairs={{1,3},{3,1},{5,7},{7,5},{9,11},{11,9},{13,15},{15,13},{17,19},{19,... | collective-permute-start | bytes 294920 | tf_op jit(solution)/shard_map/ppermute | solution.py:256
  15.8 14.5 %collective-permute-start.9 = (bf16[1152,128]{1,0:T(8,128)(2,1)S(1)}, bf16[1152,128]{1,0:T(8,128)(2,1)S(1)}, u32[]{:S(2)}, u32[]{:S(2)}) collective-permute-start(bf16[1152,128]{1,0:T(8,128)(2,1)S(1)} %constant_dynamic-update-slice_fusion.refs_6_), channel_id=1, source_target_pairs={{0,24},{4,28},{8,16},{12,20},{16,8},{20,12},{24,0},{28,4},{1,25},{... | collective-permute-start | bytes 884744 | tf_op jit(solution)/shard_map/ppermute | solution.py:253
  17.1 14.9 %collective-permute-start.8 = (bf16[1152,128]{1,0:T(8,128)(2,1)S(1)}, bf16[1152,128]{1,0:T(8,128)(2,1)S(1)}, u32[]{:S(2)}, u32[]{:S(2)}) collective-permute-start(bf16[1152,128]{1,0:T(8,128)(2,1)S(1)} %constant_dynamic-update-slice_fusion.refs_6_), channel_id=1, source_target_pairs={{0,16},{4,20},{8,24},{12,28},{16,0},{20,4},{24,8},{28,12},{1,17},{... | collective-permute-start | bytes 884744 | tf_op jit(solution)/shard_map/ppermute | solution.py:253
  17.3 14.7 %collective-permute-start.7 = (bf16[1152,128]{1,0:T(8,128)(2,1)S(1)}, bf16[1152,128]{1,0:T(8,128)(2,1)S(1)}, u32[]{:S(2)}, u32[]{:S(2)}) collective-permute-start(bf16[1152,128]{1,0:T(8,128)(2,1)S(1)} %constant_dynamic-update-slice_fusion.refs_6_), channel_id=1, source_target_pairs={{0,8},{4,12},{8,0},{12,4},{16,24},{20,28},{24,16},{28,20},{1,9},{5... | collective-permute-start | bytes 884744 | tf_op jit(solution)/shard_map/ppermute | solution.py:253
  18.5 10.2 %collective-permute-start.6 = (bf16[1152,128]{1,0:T(8,128)(2,1)S(1)}, bf16[1152,128]{1,0:T(8,128)(2,1)S(1)}, u32[]{:S(2)}, u32[]{:S(2)}) collective-permute-start(bf16[1152,128]{1,0:T(8,128)(2,1)S(1)} %constant_dynamic-update-slice_fusion.refs_6_), channel_id=1, source_target_pairs={{0,4},{4,0},{8,12},{12,8},{16,20},{20,16},{24,28},{28,24},{1,5},{5... | collective-permute-start | bytes 884744 | tf_op jit(solution)/shard_map/ppermute | solution.py:253
  21.4 7.2 %collective-permute-start.5 = (bf16[384,128]{1,0:T(8,128)(2,1)S(1)}, bf16[384,128]{1,0:T(8,128)(2,1)S(1)}, u32[]{:S(2)}, u32[]{:S(2)}) collective-permute-start(bf16[384,128]{1,0:T(8,128)(2,1)S(1)} %get-tuple-element.29.refs_0_), channel_id=1, source_target_pairs={{2,3},{3,2},{6,7},{7,6},{10,11},{11,10},{14,15},{15,14},{18,19},{1... | collective-permute-start | bytes 294920 | tf_op jit(solution)/shard_map/ppermute | solution.py:256
  28.6 6.2 %copy-start.4 = (f32[1024]{0:T(1024)S(1)}, f32[1024]{0:T(1024)}, u32[]{:S(2)}) copy-start(f32[1024]{0:T(1024)} %param.21) | copy-start | bytes 12292
  28.6 6.2 %copy-start.5 = (f32[256]{0:T(256)S(1)}, f32[256]{0:T(256)}, u32[]{:S(2)}) copy-start(f32[256]{0:T(256)} %param.23) | copy-start | bytes 3076
  28.7 6.2 %copy-start.2 = (bf16[1024,1024]{1,0:T(8,128)(2,1)S(1)}, bf16[1024,1024]{1,0:T(8,128)(2,1)}, u32[]{:S(2)}) copy-start(bf16[1024,1024]{1,0:T(8,128)(2,1)} %refs_13_.1) | copy-start | bytes 6291460
  30.3 4.5 %copy-start.3 = (bf16[1024,256]{1,0:T(8,128)(2,1)S(1)}, bf16[1024,256]{1,0:T(8,128)(2,1)}, u32[]{:S(2)}) copy-start(bf16[1024,256]{1,0:T(8,128)(2,1)} %refs_15_.1) | copy-start | bytes 1572868
  32.1 2.7 %collective-permute-start.10 = (bf16[3,1152,128]{2,1,0:T(8,128)(2,1)S(1)}, bf16[3,1152,128]{2,1,0:T(8,128)(2,1)S(1)}, u32[]{:S(2)}, u32[]{:S(2)}) collective-permute-start(bf16[3,1152,128]{2,1,0:T(8,128)(2,1)S(1)} %pad_maximum_fusion.refs_8_), channel_id=1, source_target_pairs={{0,4},{4,0},{8,12},{12,8},{16,20},{20,16},{24,28},{28,24},{1,5},{5... | collective-permute-start | bytes 2654216 | tf_op jit(solution)/shard_map/ppermute | solution.py:253
